TPU v7x, 32 devices: a whole 2x2x4 slice. The times are simulated.
32 devices in a mesh: dp: 8 (over z, y), tp: 4 (over x, core).
Axes of the slice: x: 2, y: 2, z: 4, core: 2. Of those that a mesh axis runs over, the one named last changes fastest.
Arguments:
- x_in: bfloat16 [1024, 8, 768], P('tp', 'dp'), may hold values from -6 to 6
- segments: int32 [1024, 8], P(None, 'dp'), may hold values from 0 to 4, as said below
- w_qkv: bfloat16 [2, 768, 2304], replicated, may hold values from -0.21875 to 0.21875
- w_out: bfloat16 [2, 768, 768], replicated, may hold values from -0.875 to 0.875
- mix_pre: float32 [2, 12, 12], replicated, may hold values from -1.75 to 1.75
- mix_post: float32 [2, 12, 12], replicated, may hold values from -1.75 to 1.75
- gain_attn: float32 [2, 768], replicated, may hold values from 0.5 to 1.5
- gain_ffn: float32 [2, 768], replicated, may hold values from 0.5 to 1.5
- w_in: bfloat16 [2, 768, 3072], P(None, None, 'tp'), may hold values from -0.21875 to 0.21875
- w_down: bfloat16 [2, 3072, 768], P(None, 'tp'), may hold values from -0.109375 to 0.109375
- cotangent: bfloat16 [1024, 8, 768], P('tp', 'dp'), may hold values from -6 to 6
Outputs:
- y_out: bfloat16 [1024, 8, 768], P('tp', 'dp')
- grad_x: float32 [1024, 8, 768], P('tp', 'dp')
- grad_qkv: float32 [2, 768, 2304], replicated
- grad_out: float32 [2, 768, 768], replicated
- grad_mix_pre: float32 [2, 12, 12], replicated
- grad_mix_post: float32 [2, 12, 12], replicated
- grad_gain_attn: float32 [2, 768], replicated
- grad_gain_ffn: float32 [2, 768], replicated
- grad_in: float32 [2, 768, 3072], P(None, 'dp', 'tp')
- grad_down: float32 [2, 3072, 768], P(None, 'tp', 'dp')
Inputs may be any that keep to these rules, and one draw needn't show every extreme that they name: `segments`: along each sequence the ids start at 0 and rise by one at the first position of each document; every sequence holds five documents.
All inputs are finite; a program needn't handle non-finite values.
Results may differ from a plain program's by a relative error of at most 0.035.
Values may be sent and summed in bfloat16 or wider, within the bound.
No kernel may reach another device: no remote copies, remote signals or barrier semaphores. Data moves between devices by JAX's collectives and lax.ppermute only.
A program may use at most 256 MiB of HBM per device.

v0:
```python
import functools

import jax
import jax.numpy as jnp
from jax import lax
from jax.experimental import pallas as pl
from jax.experimental.pallas import tpu as pltpu
from jax.sharding import PartitionSpec as P

LAYERS = 2
EPSILON = 1e-06
NEGATIVE = -1e30
LOG2E = 1.4426950408889634
GP = 2
VMEM = 60 * 1024 * 1024
F32 = jnp.float32
BF16 = jnp.bfloat16


def dot_nn(a, b):
    return lax.dot_general(a, b, (((1,), (0,)), ((), ())), preferred_element_type=F32)


def dot_nt(a, b):
    return lax.dot_general(a, b, (((1,), (1,)), ((), ())), preferred_element_type=F32)


def dot_tn(a, b):
    return lax.dot_general(a, b, (((0,), (0,)), ((), ())), preferred_element_type=F32)


def rms(values, gain):
    return values * lax.rsqrt(jnp.mean(values * values, -1, keepdims=True) + EPSILON) * gain


def rms_back(grad, values, gain):
    inv = lax.rsqrt(jnp.mean(values * values, -1, keepdims=True) + EPSILON)
    unit = values * inv
    scaled = grad * gain
    grad_values = (scaled - unit * jnp.mean(scaled * unit, -1, keepdims=True)) * inv
    return grad_values, jnp.sum(grad * unit, axis=0)


def whole(shape):
    return pl.BlockSpec(shape, lambda *_: (0,) * len(shape))


def layer_of(array, layer):
    shape = array.shape[1:]
    return pl.BlockSpec((1,) + shape, lambda *_: (layer,) + (0,) * len(shape))


def attn_fwd_body(blocks, heads, layer, *refs):
    n_refs = refs[:blocks]
    x_ref, wqkv_ref, wout_ref, tab_ref, gain_ref, qinfo_ref, kinfo_ref = refs[blocks : blocks + 7]
    p_ref, u_ref, q_ref, k_ref, v_ref, o_ref, xm_ref, n2_ref, bias_ref, acc_ref = refs[blocks + 7 :]
    step = pl.program_id(0)
    rows, width = x_ref.shape

    @pl.when(step == 0)
    def _():
        q_ref[...] = dot_nn(n_refs[0][...], wqkv_ref[0, :, :width]).astype(BF16)
        for r in range(blocks):
            here = pl.ds(r * rows, rows)
            k_ref[here, :] = dot_nn(n_refs[r][...], wqkv_ref[0, :, width : 2 * width]).astype(BF16)
            v_ref[here, :] = dot_nn(n_refs[r][...], wqkv_ref[0, :, 2 * width :]).astype(BF16)
        ok = (qinfo_ref[:, 1:2] == kinfo_ref[1:2, :]) & (kinfo_ref[0:1, :] <= qinfo_ref[:, 0:1])
        bias_ref[...] = jnp.where(ok, 0.0, NEGATIVE)
        acc_ref[...] = jnp.zeros_like(acc_ref)

    q = q_ref[...].astype(F32)
    for u in range(GP):
        g = step * GP + u
        qm = (q * (tab_ref[0, pl.ds(g, 1), :] * LOG2E)).astype(BF16)
        m = dot_nt(qm, k_ref[...]) + bias_ref[...]
        e = jnp.exp2(m - jnp.max(m, -1, keepdims=True))
        p = (e * (1.0 / jnp.sum(e, -1, keepdims=True))).astype(BF16)
        p_ref[u] = p
        ctx = dot_nn(p, v_ref[...])
        u_ref[u] = ctx.astype(BF16)
        acc_ref[...] += ctx * tab_ref[0, pl.ds(heads + g, 1), :]

    @pl.when(step == pl.num_programs(0) - 1)
    def _():
        o = acc_ref[...].astype(BF16)
        o_ref[...] = o
        xm = x_ref[...] + dot_nn(o, wout_ref[0])
        xm_ref[...] = xm
        n2_ref[...] = rms(xm, gain_ref[pl.ds(layer, 1), :]).astype(BF16)


def attn_fwd(layer, n_blocks, x, w_qkv, w_out, tab, gain, where):
    rows, width = x.shape
    blocks = len(n_blocks)
    heads = tab.shape[1] // 2
    keys = rows * blocks
    args = (*n_blocks, x, w_qkv, w_out, tab, gain, *where)
    in_specs = [whole(a.shape) for a in args]
    in_specs[blocks + 1] = layer_of(w_qkv, layer)
    in_specs[blocks + 2] = layer_of(w_out, layer)
    in_specs[blocks + 3] = layer_of(tab, layer)
    out = [
        ((heads, rows, keys), BF16),
        ((heads, rows, width), BF16),
        ((rows, width), BF16),
        ((keys, width), BF16),
        ((keys, width), BF16),
        ((rows, width), BF16),
        ((rows, width), F32),
        ((rows, width), BF16),
    ]
    out_specs = [whole(s) for s, _ in out]
    out_specs[0] = pl.BlockSpec((GP, rows, keys), lambda i: (i, 0, 0))
    out_specs[1] = pl.BlockSpec((GP, rows, width), lambda i: (i, 0, 0))
    return pl.pallas_call(
        functools.partial(attn_fwd_body, blocks, heads, layer),
        grid=(heads // GP,),
        in_specs=in_specs,
        out_specs=out_specs,
        out_shape=[jax.ShapeDtypeStruct(s, d) for s, d in out],
        scratch_shapes=[pltpu.VMEM((rows, keys), F32), pltpu.VMEM((rows, width), F32)],
        compiler_params=pltpu.CompilerParams(vmem_limit_bytes=VMEM),
        cost_estimate=pl.CostEstimate(
            flops=2 * rows * keys * width * heads * 2, bytes_accessed=20_000_000, transcendentals=rows * keys * heads
        ),
        name="attn_fwd",
    )(*args)


def attn_bwd_body(heads, blocks, layer, *refs):
    (ga_ref, wout_ref, q_ref, k_ref, v_ref, p_ref, u_ref, tab_ref, tabt_ref, half_ref) = refs[:10]
    wqkv_hbm, n1t_hbm, ot_hbm = refs[10:13]
    gn1_refs = refs[13 : 13 + blocks]
    (ak_ref, as_ref, bk_ref, bs_ref, zpre_ref, zpost_ref) = refs[13 + blocks : 19 + blocks]
    go_ref, got_ref, qt_ref, gq_acc, gk_acc, gv_acc, wqkv_ref, n1t_ref, ot_ref, sems = refs[19 + blocks :]
    step = pl.program_id(0)
    rows, width = q_ref.shape
    half = width // 2

    late = [
        pltpu.make_async_copy(wqkv_hbm.at[layer], wqkv_ref, sems.at[0]),
        pltpu.make_async_copy(n1t_hbm, n1t_ref, sems.at[1]),
        pltpu.make_async_copy(ot_hbm, ot_ref, sems.at[2]),
    ]

    @pl.when(step == 0)
    def _():
        for copy in late:
            copy.start()
        go = dot_nt(ga_ref[...], wout_ref[0]).astype(BF16).astype(F32)
        go_ref[...] = go
        got_ref[...] = go.T
        qt_ref[...] = q_ref[...].astype(F32).T
        gq_acc[...] = jnp.zeros_like(gq_acc)
        gk_acc[...] = jnp.zeros_like(gk_acc)
        gv_acc[...] = jnp.zeros_like(gv_acc)

    go = go_ref[...]
    q = q_ref[...].astype(F32)
    lane = lax.broadcasted_iota(jnp.int32, tabt_ref.shape[1:], 1)
    gms, ps, qms, gos = [], [], [], []
    for u in range(GP):
        g = step * GP + u
        g_mix = go * tab_ref[0, pl.ds(heads + g, 1), :]
        gp = dot_nt(g_mix.astype(BF16), v_ref[...])
        ctx = u_ref[u].astype(F32)
        zpost_ref[pl.ds(g, 1), :] = jnp.sum(ctx * go, axis=0, keepdims=True)
        delta = jnp.sum(ctx * g_mix, axis=1, keepdims=True)
        p = p_ref[u]
        gm = (p.astype(F32) * (gp - delta)).astype(BF16)
        t = dot_nn(gm, k_ref[...])
        zpre_ref[pl.ds(g, 1), :] = jnp.sum(t * q, axis=0, keepdims=True)
        gq_acc[...] += t * tab_ref[0, pl.ds(g, 1), :]
        pre_col = jnp.sum(jnp.where(lane == g, tabt_ref[0], 0.0), 1, keepdims=True)
        post_col = jnp.sum(jnp.where(lane == heads + g, tabt_ref[0], 0.0), 1, keepdims=True)
        qms.append((qt_ref[...] * pre_col).astype(BF16))
        gos.append((got_ref[...] * post_col).astype(BF16))
        gms.append(gm)
        ps.append(p)
    gk_acc[...] += dot_nn(jnp.concatenate(qms, 1), jnp.concatenate(gms, 0))
    gv_acc[...] += dot_nn(jnp.concatenate(gos, 1), jnp.concatenate(ps, 0))

    @pl.when(step == pl.num_programs(0) - 1)
    def _():
        for copy in late:
            copy.wait()
        gq = gq_acc[...].astype(BF16)
        gkt = gk_acc[...].astype(BF16)
        gvt = gv_acc[...].astype(BF16)
        ga = ga_ref[...]
        for r in range(blocks):
            here = slice(r * rows, (r + 1) * rows)
            gk = gk_acc[:, here].T.astype(BF16)
            gv = gv_acc[:, here].T.astype(BF16)
            gn1 = dot_nt(gk, wqkv_ref[:, width : 2 * width]) + dot_nt(gv, wqkv_ref[:, 2 * width :])
            if r == 0:
                gn1 = gn1 + dot_nt(gq, wqkv_ref[:, :width])
            gn1_refs[r][...] = gn1.astype(BF16)
        which = half_ref[0]
        for part, a_ref, b_ref in ((which, ak_ref, bk_ref), (1 - which, as_ref, bs_ref)):
            mine = pl.ds(pl.multiple_of(part * half, half), half)
            a_ref[:, :width] = dot_nt(n1t_ref[mine, :], gvt).astype(BF16)
            a_ref[:, width:] = dot_nn(ot_ref[mine, :], ga).astype(BF16)
            b_ref[:, :width] = dot_nn(n1t_ref[mine, :rows], gq).astype(BF16)
            b_ref[:, width:] = dot_nt(n1t_ref[mine, :], gkt).astype(BF16)


def attn_bwd(layer, blocks, ga, w_out, q, k, v, p, u, tab, tabt, half, w_qkv, n1t, ot):
    rows, width = q.shape
    keys = k.shape[0]
    heads = p.shape[0]
    args = (ga, w_out, q, k, v, p, u, tab, tabt, half, w_qkv, n1t, ot)
    in_specs = [whole(a.shape) for a in args]
    in_specs[1] = layer_of(w_out, layer)
    in_specs[5] = pl.BlockSpec((GP, rows, keys), lambda i: (i, 0, 0))
    in_specs[6] = pl.BlockSpec((GP, rows, width), lambda i: (i, 0, 0))
    in_specs[7] = layer_of(tab, layer)
    in_specs[8] = layer_of(tabt, layer)
    in_specs[9] = pl.BlockSpec(memory_space=pltpu.SMEM)
    in_specs[10:13] = [pl.BlockSpec(memory_space=pl.ANY)] * 3
    out = (
        [((rows, width), BF16)] * blocks
        + [((width // 2, 2 * width), BF16)] * 4
        + [((heads, width), F32)] * 2
    )
    res = pl.pallas_call(
        functools.partial(attn_bwd_body, heads, blocks, layer),
        grid=(heads // GP,),
        in_specs=in_specs,
        out_specs=[whole(s) for s, _ in out],
        out_shape=[jax.ShapeDtypeStruct(s, d) for s, d in out],
        scratch_shapes=[
            pltpu.VMEM((rows, width), F32),
            pltpu.VMEM((width, rows), F32),
            pltpu.VMEM((width, rows), F32),
            pltpu.VMEM((rows, width), F32),
            pltpu.VMEM((width, keys), F32),
            pltpu.VMEM((width, keys), F32),
            pltpu.VMEM(w_qkv.shape[1:], BF16),
            pltpu.VMEM(n1t.shape, BF16),
            pltpu.VMEM(ot.shape, BF16),
            pltpu.SemaphoreType.DMA((3,)),
        ],
        compiler_params=pltpu.CompilerParams(vmem_limit_bytes=VMEM),
        cost_estimate=pl.CostEstimate(
            flops=2 * rows * keys * width * heads * 4 * 2, bytes_accessed=20_000_000, transcendentals=0
        ),
        name="attn_bwd",
    )(*args)
    return res[:blocks], res[blocks : blocks + 4], res[blocks + 4], res[blocks + 5]


def expand_body(*refs):
    which_ref, am_ref, ao_ref, bm_ref, bo_ref = refs[:5]
    qkv_ref, out_ref = refs[-2:]
    step = pl.program_id(0)
    width = out_ref.shape[2]
    other = (step // (pl.num_programs(0) // 2)) != which_ref[0]

    def write(a_ref, b_ref):
        qkv_ref[0, :, : 2 * width] = b_ref[...].astype(F32)
        qkv_ref[0, :, 2 * width :] = a_ref[:, :width].astype(F32)
        out_ref[0] = a_ref[:, width:].astype(F32)

    @pl.when(other)
    def _():
        write(ao_ref, bo_ref)

    @pl.when(jnp.logical_not(other))
    def _():
        write(am_ref, bm_ref)


def expand(layer, a_mine, a_other, b_mine, b_other, which, before=None):
    half, width2 = a_mine.shape
    width = width2 // 2
    steps = 8
    per = 2 * half // steps
    block = pl.BlockSpec((per, width2), lambda i: (i % (steps // 2), 0))
    in_specs = [pl.BlockSpec(memory_space=pltpu.SMEM)] + [block] * 4
    args = [which, a_mine, a_other, b_mine, b_other]
    aliases = {}
    if before is not None:
        in_specs += [pl.BlockSpec(memory_space=pl.ANY)] * 2
        args += before
        aliases = {5: 0, 6: 1}
    return pl.pallas_call(
        expand_body,
        grid=(steps,),
        in_specs=in_specs,
        out_specs=[
            pl.BlockSpec((1, per, 3 * width), lambda i: (layer, i, 0)),
            pl.BlockSpec((1, per, width), lambda i: (layer, i, 0)),
        ],
        out_shape=[
            jax.ShapeDtypeStruct((LAYERS, 2 * half, 3 * width), F32),
            jax.ShapeDtypeStruct((LAYERS, 2 * half, width), F32),
        ],
        input_output_aliases=aliases,
        cost_estimate=pl.CostEstimate(flops=0, bytes_accessed=20_000_000, transcendentals=0),
        name="expand",
    )(*args)


def ffn_fwd_body(blocks, *refs):
    n_refs = refs[:blocks]
    win_ref, wdown_ref = refs[blocks : blocks + 2]
    out_refs = refs[blocks + 2 : 2 * blocks + 2]
    hid_ref, dgelu_ref = refs[2 * blocks + 2 :]
    rows = n_refs[0].shape[0]
    for r in range(blocks):
        here = pl.ds(r * rows, rows)
        pre = dot_nn(n_refs[r][...], win_ref[0])
        cdf = 0.5 + 0.5 * lax.erf(pre * (0.5**0.5))
        hid = (pre * cdf).astype(BF16)
        hid_ref[here, :] = hid
        density = jnp.exp2(pre * pre * (-0.5 * LOG2E)) * 0.3989422804014327
        dgelu_ref[here, :] = (cdf + pre * density).astype(BF16)
        out_refs[r][...] = dot_nn(hid, wdown_ref[0]).astype(BF16)


def ffn_fwd(layer, n_blocks, w_in, w_down):
    blocks = len(n_blocks)
    rows, width = n_blocks[0].shape
    hidden = w_in.shape[2]
    args = (*n_blocks, w_in, w_down)
    in_specs = [whole(a.shape) for a in args]
    in_specs[blocks] = layer_of(w_in, layer)
    in_specs[blocks + 1] = layer_of(w_down, layer)
    out = [((rows, width), BF16)] * blocks + [((rows * blocks, hidden), BF16)] * 2
    res = pl.pallas_call(
        functools.partial(ffn_fwd_body, blocks),
        grid=(1,),
        in_specs=in_specs,
        out_specs=[whole(s) for s, _ in out],
        out_shape=[jax.ShapeDtypeStruct(s, d) for s, d in out],
        compiler_params=pltpu.CompilerParams(vmem_limit_bytes=VMEM),
        cost_estimate=pl.CostEstimate(
            flops=4 * rows * blocks * width * hidden, bytes_accessed=6_000_000, transcendentals=rows * blocks * hidden
        ),
        name="ffn_fwd",
    )(*args)
    return res[:blocks], res[blocks], res[blocks + 1]


def ffn_bwd_body(blocks, *refs):
    g_refs = refs[:blocks]
    dgelu_ref, win_ref, wdown_ref = refs[blocks : blocks + 3]
    out_refs = refs[blocks + 3 : 2 * blocks + 3]
    gpre_ref = refs[2 * blocks + 3]
    rows = g_refs[0].shape[0]
    for r in range(blocks):
        here = pl.ds(r * rows, rows)
        gh = dot_nt(g_refs[r][...], wdown_ref[0])
        gpre = (gh * dgelu_ref[here, :].astype(F32)).astype(BF16)
        gpre_ref[here, :] = gpre
        out_refs[r][...] = dot_nt(gpre, win_ref[0]).astype(BF16)


def ffn_bwd(layer, g_blocks, dgelu, w_in, w_down):
    blocks = len(g_blocks)
    rows, width = g_blocks[0].shape
    hidden = w_in.shape[2]
    args = (*g_blocks, dgelu, w_in, w_down)
    in_specs = [whole(a.shape) for a in args]
    in_specs[blocks + 1] = layer_of(w_in, layer)
    in_specs[blocks + 2] = layer_of(w_down, layer)
    out = [((rows, width), BF16)] * blocks + [((rows * blocks, hidden), BF16)]
    res = pl.pallas_call(
        functools.partial(ffn_bwd_body, blocks),
        grid=(1,),
        in_specs=in_specs,
        out_specs=[whole(s) for s, _ in out],
        out_shape=[jax.ShapeDtypeStruct(s, d) for s, d in out],
        compiler_params=pltpu.CompilerParams(vmem_limit_bytes=VMEM),
        cost_estimate=pl.CostEstimate(
            flops=4 * rows * blocks * width * hidden, bytes_accessed=6_000_000, transcendentals=0
        ),
        name="ffn_bwd",
    )(*args)
    return res[:blocks], res[blocks]


def swap(value, axis, bit):
    size = lax.axis_size(axis)
    return lax.ppermute(value, axis, [(i, i ^ bit) for i in range(size)])


def gather_blocks(value):
    blocks = {0: value}
    bit = lax.axis_size("tp") // 2
    while bit:
        for r in list(blocks):
            blocks[r | bit] = swap(blocks[r], "tp", bit)
        bit //= 2
    return [blocks[r] for r in range(len(blocks))]


def scatter_sum(blocks):
    blocks = list(blocks)
    bit = 1
    while bit < lax.axis_size("tp"):
        size = len(blocks)
        keep = [blocks[r] for r in range(size) if not r & 1]
        sent = [swap(blocks[r], "tp", bit) for r in range(size) if r & 1]
        blocks = [a.astype(F32) + b.astype(F32) for a, b in zip(keep, sent)]
        bit *= 2
        if bit < lax.axis_size("tp"):
            blocks = [blocks[0]] + [b.astype(BF16) for b in blocks[1:]]
    return blocks[0]


def halve(part, axis, bit):
    mine = (lax.axis_index(axis) // bit) & 1
    pair = part.reshape(2, part.shape[0] // 2, part.shape[1])
    sent = lax.dynamic_index_in_dim(pair, 1 - mine, 0, keepdims=False)
    kept = lax.dynamic_index_in_dim(pair, mine, 0, keepdims=False)
    return (kept.astype(F32) + swap(sent, axis, bit).astype(F32)).astype(BF16)


def double(part, axis, bit):
    first = ((lax.axis_index(axis) // bit) & 1) == 0
    got = swap(part, axis, bit)
    return jnp.concatenate([jnp.where(first, part, got), jnp.where(first, got, part)], 0)


def steps_of(axis):
    return [(axis, 1 << i) for i in range(lax.axis_size(axis).bit_length() - 1)]


def sum_halves(keep_a, send_a, keep_b, send_b):
    first, *tp_rest = steps_of("tp")
    dp_first, *dp_rest = steps_of("dp")
    orders = (tp_rest + [dp_first] + dp_rest, [dp_first] + tp_rest + dp_rest)
    parts = [
        (keep.astype(F32) + swap(send, *first).astype(F32)).astype(BF16)
        for keep, send in ((keep_a, send_a), (keep_b, send_b))
    ]
    for stage in range(len(orders[0])):
        parts = [halve(part, *order[stage]) for part, order in zip(parts, orders)]
    for stage in range(len(orders[0]) - 1, -1, -1):
        parts = [double(part, *order[stage]) for part, order in zip(parts, orders)]
    others = [swap(part, *first) for part in parts]
    return parts[0], others[0], parts[1], others[1]


def butterfly(value):
    for axis in ("tp", "dp"):
        bit = 1
        while bit < lax.axis_size(axis):
            value = value + swap(value, axis, bit)
            bit *= 2
    return value


def on_device(
    x_in, segments, w_qkv, w_out, mix_pre, mix_post, gain_attn, gain_ffn, w_in, w_down, cotangent
):
    rows, _, width = x_in.shape
    heads = mix_pre.shape[1]
    head_size = width // heads
    tp_size = lax.axis_size("tp")
    dp_size = lax.axis_size("dp")
    tp_index = lax.axis_index("tp")
    seg = segments[:, 0]
    span = jnp.arange(rows, dtype=jnp.int32)
    kpos = jnp.concatenate([(tp_index ^ r) * rows + span for r in range(tp_size)])
    kseg = jnp.concatenate([lax.dynamic_slice_in_dim(seg, (tp_index ^ r) * rows, rows, 0) for r in range(tp_size)])
    kinfo = jnp.pad(jnp.stack([kpos, kseg]), ((0, 6), (0, 0)))
    where = (kinfo[:, :rows].T, kinfo)

    tab = jnp.concatenate([jnp.swapaxes(mix_pre, 1, 2) * (head_size**-0.5), mix_post], 1)
    tabt = jnp.pad(jnp.repeat(jnp.swapaxes(tab, 1, 2), head_size, axis=1), ((0, 0), (0, 0), (0, 128 - 2 * heads)))
    tab = jnp.repeat(tab, head_size, axis=2)

    grad_last = gather_blocks(cotangent[:, 0])
    stream = x_in[:, 0].astype(F32)
    kept = []
    for layer in range(LAYERS):
        n1_blocks = gather_blocks(rms(stream, gain_attn[layer]).astype(BF16))
        p, u, q, k, v, o, middle, n2 = attn_fwd(
            layer,
            n1_blocks,
            stream,
            w_qkv,
            w_out,
            tab,
            gain_ffn,
            where,
        )
        n2_blocks = gather_blocks(n2)
        half = tp_size // 2
        out_a, hid_a, dgelu_a = ffn_fwd(layer, n2_blocks[:half], w_in, w_down)
        out_b, hid_b, dgelu_b = ffn_fwd(layer, n2_blocks[half:], w_in, w_down)
        kept.append((stream, n1_blocks, p, u, q, k, v, o, middle, n2_blocks, hid_a, hid_b, dgelu_a, dgelu_b))
        stream = middle + scatter_sum([*out_a, *out_b])
    y_out = stream.astype(BF16)

    grad_flow = cotangent[:, 0].astype(F32)
    small = [None] * LAYERS
    replicated = None
    sharded = [None] * LAYERS
    for layer in range(LAYERS - 1, -1, -1):
        stream, n1_blocks, p, u, q, k, v, o, middle, n2_blocks, hid_a, hid_b, dgelu_a, dgelu_b = kept[layer]
        gf_blocks = grad_last if layer == LAYERS - 1 else gather_blocks(grad_flow.astype(BF16))
        gn2_a, gpre_a = ffn_bwd(layer, gf_blocks[:half], dgelu_a, w_in, w_down)
        gn2_b, gpre_b = ffn_bwd(layer, gf_blocks[half:], dgelu_b, w_in, w_down)
        gf_all = jnp.concatenate(gf_blocks, 0)
        n2_all = jnp.concatenate(n2_blocks, 0)
        gpre = jnp.concatenate([gpre_a, gpre_b], 0)
        hid = jnp.concatenate([hid_a, hid_b], 0)
        grad_win = dot_tn(n2_all, gpre).astype(BF16)
        grad_wdown_t = dot_tn(gf_all, hid).astype(BF16)
        per = width // dp_size
        packed = jnp.concatenate(
            [grad_win.reshape(dp_size, per, -1), grad_wdown_t.reshape(dp_size, per, -1)], 1
        ).reshape(2 * width, -1)
        summed = lax.psum_scatter(packed, "dp", scatter_dimension=0, tiled=True).astype(F32)
        sharded[layer] = (summed[:per], summed[per:].T)

        gn2 = scatter_sum([*gn2_a, *gn2_b]).astype(BF16).astype(F32)
        grad_norm, grad_gffn = rms_back(gn2, middle, gain_ffn[layer])
        grad_middle = grad_flow + grad_norm
        ga = grad_middle.astype(BF16)
        core = tp_index & 1 if layer == 0 else jnp.int32(0)
        parts, grads, zpre, zpost = attn_bwd(
            layer,
            tp_size,
            ga,
            w_out,
            q,
            k,
            v,
            p,
            u,
            tab,
            tabt,
            core[None],
            w_qkv,
            jnp.concatenate(n1_blocks, 0).T,
            o.T,
        )
        if layer == 0:
            keep_a, send_a, keep_b, send_b = grads
            replicated = expand(layer, *sum_halves(keep_a, send_a, keep_b, send_b), core[None], replicated)
        else:
            keep_a, send_a, keep_b, send_b = lax.psum(tuple(grads), ("dp", "tp"))
            replicated = expand(layer, keep_a, send_a, keep_b, send_b, core[None], replicated)
        gn1 = scatter_sum(parts).astype(BF16).astype(F32)
        grad_norm, grad_gattn = rms_back(gn1, stream, gain_attn[layer])
        grad_flow = grad_middle + grad_norm
        grad_mpre = jnp.sum(zpre.reshape(heads, heads, head_size), -1).T * (head_size**-0.5)
        grad_mpost = jnp.sum(zpost.reshape(heads, heads, head_size), -1)
        small[layer] = (grad_mpre, grad_mpost, grad_gattn, grad_gffn)

    mixes = jnp.concatenate([a.reshape(-1) for s in small for a in s[:2]])
    count = mixes.shape[0]
    mix_rows = -(-count // width)
    flat = jnp.concatenate(
        [jnp.pad(mixes, (0, mix_rows * width - count)).reshape(mix_rows, width)]
        + [g[None] for s in small for g in s[2:]]
    )
    flat = jnp.pad(flat, ((0, -flat.shape[0] % 8), (0, 0)))
    flat = butterfly(flat)
    mixes = flat[:mix_rows].reshape(-1)[:count].reshape(LAYERS, 2, heads, heads)
    gains = flat[mix_rows : mix_rows + 2 * LAYERS].reshape(LAYERS, 2, width)
    return (
        y_out[:, None],
        grad_flow[:, None],
        *replicated,
        mixes[:, 0],
        mixes[:, 1],
        gains[:, 0],
        gains[:, 1],
        jnp.stack([s[0] for s in sharded]),
        jnp.stack([s[1] for s in sharded]),
    )


def solution(mesh):
    in_specs = (
        P("tp", "dp", None),
        P(None, "dp"),
        P(),
        P(),
        P(),
        P(),
        P(),
        P(),
        P(None, None, "tp"),
        P(None, "tp", None),
        P("tp", "dp", None),
    )
    out_specs = (
        P("tp", "dp", None),
        P("tp", "dp", None),
        P(),
        P(),
        P(),
        P(),
        P(),
        P(),
        P(None, "dp", "tp"),
        P(None, "tp", "dp"),
    )
    return jax.shard_map(
        on_device, mesh=mesh, in_specs=in_specs, out_specs=out_specs, check_vma=False
    )
```

profile of v0, /device:TPU:0, one launch (start us, length us, event | category | flops | bytes accessed | tf_op | source)
XLA Modules:
  0.0 559.9 jit_solution(12908534613834257093)
XLA Ops:
  14.2 8.3 %collective-permute-done.1 = bf16[256,768]{0,1:T(8,128)(2,1)S(1)} collective-permute-done((bf16[256,768]{0,1:T(8,128)(2,1)S(1)}, bf16[256,768]{0,1:T(8,128)(2,1)S(1)}, u32[]{:S(2)}, u32[]{:S(2)}) %collective-permute-start.1) | collective-permute-done | bytes 393248 | tf_op jit(solution)/shard_map/ppermute | solution.py:386
  29.8 27.2 %attn_fwd.2 = (bf16[12,256,1024]{2,1,0:T(8,128)(2,1)}, bf16[12,256,768]{2,1,0:T(8,128)(2,1)}, bf16[256,768]{1,0:T(8,128)(2,1)}, bf16[1024,768]{1,0:T(8,128)(2,1)...) custom-call(bf16[256,768]{1,0:T(8,128)(2,1)} %copy.134.refs_0_, ...), custom_call_target="tpu_custom_call" | custom-call | flops 9663676416 | bytes 20000000 | tf_op jit(solution)/shard_map/attn_fwd/pallas_call | solution.py:115
  58.8 10.0 %collective-permute-done.5.refs_0_ = bf16[256,768]{1,0:T(8,128)(2,1)S(1)} collective-permute-done((bf16[256,768]{1,0:T(8,128)(2,1)}, bf16[256,768]{1,0:T(8,128)(2,1)S(1)}, u32[]{:S(2)}, u32[]{:S(2)}) %collective-permute-start.5) | collective-permute-done | bytes 393248 | tf_op jit(solution)/shard_map/ppermute | solution.py:386
  88.7 9.2 %collective-permute-done.8 = bf16[256,768]{0,1:T(8,128)(2,1)S(1)} collective-permute-done((bf16[256,768]{0,1:T(8,128)(2,1)}, bf16[256,768]{0,1:T(8,128)(2,1)S(1)}, u32[]{:S(2)}, u32[]{:S(2)}) %collective-permute-start.8) | collective-permute-done | bytes 393248 | tf_op jit(solution)/shard_map/ppermute | solution.py:386
  100.4 8.6 %collective-permute-done.10 = bf16[256,768]{0,1:T(8,128)(2,1)S(1)} collective-permute-done((bf16[256,768]{0,1:T(8,128)(2,1)S(1)}, bf16[256,768]{0,1:T(8,128)(2,1)S(1)}, u32[]{:S(2)}, u32[]{:S(2)}) %collective-permute-start.10) | collective-permute-done | bytes 393248 | tf_op jit(solution)/shard_map/ppermute | solution.py:386
  113.9 26.9 %attn_fwd.3 = (bf16[12,256,1024]{2,1,0:T(8,128)(2,1)}, bf16[12,256,768]{2,1,0:T(8,128)(2,1)}, bf16[256,768]{1,0:T(8,128)(2,1)}, bf16[1024,768]{1,0:T(8,128)(2,1)...) custom-call(bf16[256,768]{1,0:T(8,128)(2,1)} %copy.145.refs_0_, ...), custom_call_target="tpu_custom_call" | custom-call | flops 9663676416 | bytes 20000000 | tf_op jit(solution)/shard_map/attn_fwd/pallas_call | solution.py:115
  143.1 9.9 %collective-permute-done.14.refs_0_ = bf16[256,768]{1,0:T(8,128)(2,1)} collective-permute-done((bf16[256,768]{1,0:T(8,128)(2,1)}, bf16[256,768]{1,0:T(8,128)(2,1)}, u32[]{:S(2)}, u32[]{:S(2)}) %collective-permute-start.14) | collective-permute-done | bytes 393248 | tf_op jit(solution)/shard_map/ppermute | solution.py:386
  153.6 7.4 %collective-permute-done.20 = bf16[256,768]{0,1:T(8,128)(2,1)S(1)} collective-permute-done((bf16[256,768]{0,1:T(8,128)(2,1)S(1)}, bf16[256,768]{0,1:T(8,128)(2,1)S(1)}, u32[]{:S(2)}, u32[]{:S(2)}) %collective-permute-start.20) | collective-permute-done | bytes 393248 | tf_op jit(solution)/shard_map/ppermute | solution.py:386
  195.7 4.7 ffn_bwd.4
  210.3 8.8 %collective-permute-done.23 = bf16[256,768]{0,1:T(8,128)(2,1)S(1)} collective-permute-done((bf16[256,768]{0,1:T(8,128)(2,1)S(1)}, bf16[256,768]{0,1:T(8,128)(2,1)S(1)}, u32[]{:S(2)}, u32[]{:S(2)}) %collective-permute-start.23) | collective-permute-done | bytes 393248 | tf_op jit(solution)/shard_map/ppermute | solution.py:386
  224.0 35.5 %attn_bwd.2 = (bf16[256,768]{1,0:T(8,128)(2,1)}, bf16[256,768]{1,0:T(8,128)(2,1)}, bf16[256,768]{1,0:T(8,128)(2,1)}, bf16[256,768]{1,0:T(8,128)(2,1)}, bf16[384,...) custom-call(bf16[256,768]{1,0:T(8,128)(2,1)} %copy.163.refs_0_, ...), custom_call_target="tpu_custom_call" | custom-call | flops 38654705664 | bytes 20000000 | tf_op jit(solution)/shard_map/attn_bwd/pallas_call | solution.py:226
  268.0 10.6 %collective-permute-done.26 = bf16[256,768]{0,1:T(8,128)(2,1)} collective-permute-done((bf16[256,768]{0,1:T(8,128)(2,1)}, bf16[256,768]{0,1:T(8,128)(2,1)}, u32[]{:S(2)}, u32[]{:S(2)}) %collective-permute-start.26) | collective-permute-done | bytes 393248 | tf_op jit(solution)/shard_map/ppermute | solution.py:386
  282.4 13.3 %collective-permute-done.29 = bf16[256,768]{0,1:T(8,128)(2,1)} collective-permute-done((bf16[256,768]{0,1:T(8,128)(2,1)}, bf16[256,768]{0,1:T(8,128)(2,1)}, u32[]{:S(2)}, u32[]{:S(2)}) %collective-permute-start.29) | collective-permute-done | bytes 393248 | tf_op jit(solution)/shard_map/ppermute | solution.py:386
  307.1 4.7 ffn_bwd.7
  321.0 4.7 ffn_bwd.6
  347.8 35.7 %attn_bwd.3 = (bf16[256,768]{1,0:T(8,128)(2,1)}, bf16[256,768]{1,0:T(8,128)(2,1)}, bf16[256,768]{1,0:T(8,128)(2,1)}, bf16[256,768]{1,0:T(8,128)(2,1)}, bf16[384,...) custom-call(bf16[256,768]{1,0:T(8,128)(2,1)} %copy.178.refs_0_, ...), custom_call_target="tpu_custom_call" | custom-call | flops 38654705664 | bytes 20000000 | tf_op jit(solution)/shard_map/attn_bwd/pallas_call | solution.py:226
  396.1 9.1 %collective-permute-done.35 = bf16[256,768]{0,1:T(8,128)(2,1)S(1)} collective-permute-done((bf16[256,768]{0,1:T(8,128)(2,1)S(1)}, bf16[256,768]{0,1:T(8,128)(2,1)S(1)}, u32[]{:S(2)}, u32[]{:S(2)}) %collective-permute-start.35) | collective-permute-done | bytes 393248 | tf_op jit(solution)/shard_map/ppermute | solution.py:386
  417.2 10.4 %all-reduce.7.cloned.1.call-done = (bf16[384,1536]{1,0:T(8,128)(2,1)}, bf16[384,1536]{1,0:T(8,128)(2,1)}, bf16[384,1536]{1,0:T(8,128)(2,1)}, bf16[384,1536]{1,0:T(8,128)(2,1)}) async-done(((bf16[384,1536]{1,0:T(8,128)(2,1)}, bf16[384,1536]{1,0:T(8,128)(2,1)}, bf16[384,1536]{1,0:T(8,128)(2,1)}, bf16[384,1536]{1,0:T(8,128)(2,1)}), (bf16[384,1536]{1,0:T(8,128)(2,1)}, bf16[384,1536]{1,0:T(8,128)(2,1)}, ...) | async-done | bytes 4718608 | tf_op jit(solution)/shard_map/psum | solution.py:547
  427.6 9.5 %expand.2 = (f32[2,768,2304]{2,1,0:T(8,128)}, f32[2,768,768]{2,1,0:T(8,128)}) custom-call(s32[1]{0:T(128)} %constant.144.clone.1.refs_9_.refs_0_, bf16[384,1536]{1,0:T(8,128)(2,1)} %get-tuple-element.188.refs_1_, bf16[384,1536]{1,0:T(8,128)(2,1)} %get-tuple-element.189.refs_2_, bf16[384,1536]{1,0:T(8,128)(2,1)} %get-tuple-element.190.refs_3_, ...), custom_call_target="tpu_custom_call" | custom-call | bytes 20000000 | tf_op jit(solution)/shard_map/expand/pallas_call | solution.py:287
  455.7 11.2 %collective-permute-done.37 = bf16[192,1536]{1,0:T(8,128)(2,1)S(1)} collective-permute-done((bf16[192,1536]{1,0:T(8,128)(2,1)S(1)}, bf16[192,1536]{1,0:T(8,128)(2,1)S(1)}, u32[]{:S(2)}, u32[]{:S(2)}) %collective-permute-start.37) | collective-permute-done | bytes 589856 | tf_op jit(solution)/shard_map/ppermute | solution.py:386
  467.3 7.0 %collective-permute-done.47 = bf16[192,1536]{1,0:T(8,128)(2,1)S(1)} collective-permute-done((bf16[192,1536]{1,0:T(8,128)(2,1)S(1)}, bf16[192,1536]{1,0:T(8,128)(2,1)S(1)}, u32[]{:S(2)}, u32[]{:S(2)}) %collective-permute-start.47) | collective-permute-done | bytes 589856 | tf_op jit(solution)/shard_map/ppermute | solution.py:386
  481.4 9.1 %collective-permute-done.39 = bf16[48,1536]{1,0:T(8,128)(2,1)S(1)} collective-permute-done((bf16[48,1536]{1,0:T(8,128)(2,1)S(1)}, bf16[48,1536]{1,0:T(8,128)(2,1)S(1)}, u32[]{:S(2)}, u32[]{:S(2)}) %collective-permute-start.39) | collective-permute-done | bytes 147488 | tf_op jit(solution)/shard_map/ppermute | solution.py:386
  525.7 9.3 %collective-permute-done.44 = bf16[192,1536]{1,0:T(8,128)(2,1)S(1)} collective-permute-done((bf16[192,1536]{1,0:T(8,128)(2,1)S(1)}, bf16[192,1536]{1,0:T(8,128)(2,1)S(1)}, u32[]{:S(2)}, u32[]{:S(2)}) %collective-permute-start.44) | collective-permute-done | bytes 589856 | tf_op jit(solution)/shard_map/ppermute | solution.py:386
  542.8 9.4 %expand.3 = (f32[2,768,2304]{2,1,0:T(8,128)}, f32[2,768,768]{2,1,0:T(8,128)}) custom-call(s32[1]{0:T(128)} %bitcast.17.refs_9_.refs_0_, bf16[384,1536]{1,0:T(8,128)(2,1)} %copy-done, bf16[384,1536]{1,0:T(8,128)(2,1)} %collective-permute-done.45.refs_2_, bf16[384,1536]{1,0:T(8,128)(2,1)} %copy-done.1, ...), custom_call_target="tpu_custom_call", output_to_operand_aliasing={{0}: (5, {}), {1}: (6, {})} | custom-call | bytes 20000000 | tf_op jit(solution)/shard_map/expand/pallas_call | solution.py:287
  (416 shorter events, 242.5 us)
Async XLA Ops:
  8.0 419.5 %all-reduce.7.cloned.1.call-start = ((), (), s32[]{:S(2)}) async-start(), calls=%async_computation.4 | async-start | bytes 9437184 | tf_op jit(solution)/shard_map/psum | solution.py:547
  13.4 14.5 %collective-permute-start = (bf16[256,768]{0,1:T(8,128)(2,1)S(1)}, bf16[256,768]{0,1:T(8,128)(2,1)S(1)}, u32[]{:S(2)}, u32[]{:S(2)}) collective-permute-start(bf16[256,768]{0,1:T(8,128)(2,1)S(1)} %multiply_convert_fusion.1), channel_id=1, source_target_pairs={{0,1},{1,0},{2,3},{3,2},{4,5},{5,4},{6,7},{7,6},{8,9},{9,8},{10,11... | collective-permute-start | bytes 1179656 | tf_op jit(solution)/shard_map/ppermute | solution.py:386
  142.8 18.2 %collective-permute-start.20 = (bf16[256,768]{0,1:T(8,128)(2,1)S(1)}, bf16[256,768]{0,1:T(8,128)(2,1)S(1)}, u32[]{:S(2)}, u32[]{:S(2)}) collective-permute-start(bf16[256,768]{0,1:T(8,128)(2,1)S(1)} %bitcast.128), channel_id=1, source_target_pairs={{0,2},{1,3},{2,0},{3,1},{4,6},{5,7},{6,4},{7,5},{8,10},{9,11},{10,... | collective-permute-start | bytes 1179656 | tf_op jit(solution)/shard_map/ppermute | solution.py:386
  153.1 18.6 %collective-permute-start.18 = (bf16[256,768]{0,1:T(8,128)(2,1)S(1)}, bf16[256,768]{0,1:T(8,128)(2,1)}, u32[]{:S(2)}, u32[]{:S(2)}) collective-permute-start(bf16[256,768]{0,1:T(8,128)(2,1)S(1)} %bitcast.129), channel_id=1, source_target_pairs={{0,1},{1,0},{2,3},{3,2},{4,5},{5,4},{6,7},{7,6},{8,9},{9,8},{10,11... | collective-permute-start | bytes 1179656 | tf_op jit(solution)/shard_map/ppermute | solution.py:386
  161.0 12.6 %collective-permute-start.21 = (bf16[256,768]{0,1:T(8,128)(2,1)S(1)}, bf16[256,768]{0,1:T(8,128)(2,1)}, u32[]{:S(2)}, u32[]{:S(2)}) collective-permute-start(bf16[256,768]{0,1:T(8,128)(2,1)S(1)} %collective-permute-done.20), channel_id=1, source_target_pairs={{0,1},{1,0},{2,3},{3,2},{4,5},{5,4},{6,7},{7,6},{8,9},{9,8},{10,11... | collective-permute-start | bytes 1179656 | tf_op jit(solution)/shard_map/ppermute | solution.py:386
  161.0 14.5 %collective-permute-start.12 = (bf16[256,768]{1,0:T(8,128)(2,1)}, bf16[256,768]{1,0:T(8,128)(2,1)}, u32[]{:S(2)}, u32[]{:S(2)}) collective-permute-start(bf16[256,768]{1,0:T(8,128)(2,1)} %get-tuple-element.85.refs_0_), channel_id=1, source_target_pairs={{0,1},{1,0},{2,3},{3,2},{4,5},{5,4},{6,7},{7,6},{8,9},{9,8},{10,11... | collective-permute-start | bytes 1179656 | tf_op jit(solution)/shard_map/ppermute | solution.py:386
  166.8 20.5 %collective-permute-start.16 = (bf16[256,768]{1,0:T(8,128)(2,1)}, bf16[256,768]{1,0:T(8,128)(2,1)}, u32[]{:S(2)}, u32[]{:S(2)}) collective-permute-start(bf16[256,768]{1,0:T(8,128)(2,1)} %get-tuple-element.89), channel_id=1, source_target_pairs={{0,1},{1,0},{2,3},{3,2},{4,5},{5,4},{6,7},{7,6},{8,9},{9,8},{10,11... | collective-permute-start | bytes 1179656 | tf_op jit(solution)/shard_map/ppermute | solution.py:386
  180.2 27.9 %collective-permute-start.13 = (bf16[256,768]{1,0:T(8,128)(2,1)}, bf16[256,768]{1,0:T(8,128)(2,1)}, u32[]{:S(2)}, u32[]{:S(2)}) collective-permute-start(bf16[256,768]{1,0:T(8,128)(2,1)} %get-tuple-element.87), channel_id=1, source_target_pairs={{0,1},{1,0},{2,3},{3,2},{4,5},{5,4},{6,7},{7,6},{8,9},{9,8},{10,11... | collective-permute-start | bytes 1179656 | tf_op jit(solution)/shard_map/ppermute | solution.py:386
  187.3 19.1 %collective-permute-start.22 = (bf16[256,768]{0,1:T(8,128)(2,1)}, bf16[256,768]{0,1:T(8,128)(2,1)}, u32[]{:S(2)}, u32[]{:S(2)}) collective-permute-start(bf16[256,768]{0,1:T(8,128)(2,1)} %copy.159), channel_id=1, source_target_pairs={{0,1},{1,0},{2,3},{3,2},{4,5},{5,4},{6,7},{7,6},{8,9},{9,8},{10,11... | collective-permute-start | bytes 1179656 | tf_op jit(solution)/shard_map/ppermute | solution.py:386
  189.3 18.8 %collective-permute-start.17 = (bf16[256,768]{1,0:T(8,128)(2,1)}, bf16[256,768]{1,0:T(8,128)(2,1)}, u32[]{:S(2)}, u32[]{:S(2)}) collective-permute-start(bf16[256,768]{1,0:T(8,128)(2,1)} %add_convert_fusion.11), channel_id=1, source_target_pairs={{0,2},{1,3},{2,0},{3,1},{4,6},{5,7},{6,4},{7,5},{8,10},{9,11},{10,... | collective-permute-start | bytes 1179656 | tf_op jit(solution)/shard_map/ppermute | solution.py:386
  266.1 12.5 %collective-permute-start.26 = (bf16[256,768]{0,1:T(8,128)(2,1)}, bf16[256,768]{0,1:T(8,128)(2,1)}, u32[]{:S(2)}, u32[]{:S(2)}) collective-permute-start(bf16[256,768]{0,1:T(8,128)(2,1)} %add_convert_fusion.7), channel_id=1, source_target_pairs={{0,2},{1,3},{2,0},{3,1},{4,6},{5,7},{6,4},{7,5},{8,10},{9,11},{10,... | collective-permute-start | bytes 1179656 | tf_op jit(solution)/shard_map/ppermute | solution.py:386
  267.6 271.4 %reduce-scatter.5.cloned.1.call-start = ((), (), s32[]{:S(2)}) async-start(), calls=%async_computation.3 | async-start | bytes 2654208 | tf_op jit(solution)/shard_map/reduce_scatter | solution.py:518
  282.3 13.5 %collective-permute-start.29 = (bf16[256,768]{0,1:T(8,128)(2,1)}, bf16[256,768]{0,1:T(8,128)(2,1)}, u32[]{:S(2)}, u32[]{:S(2)}) collective-permute-start(bf16[256,768]{0,1:T(8,128)(2,1)} %fusion.104), channel_id=1, source_target_pairs={{0,2},{1,3},{2,0},{3,1},{4,6},{5,7},{6,4},{7,5},{8,10},{9,11},{10,... | collective-permute-start | bytes 1179656 | tf_op jit(solution)/shard_map/ppermute | solution.py:386
  302.7 17.3 %collective-permute-start.27 = (bf16[256,768]{0,1:T(8,128)(2,1)}, bf16[256,768]{0,1:T(8,128)(2,1)S(1)}, u32[]{:S(2)}, u32[]{:S(2)}) collective-permute-start(bf16[256,768]{0,1:T(8,128)(2,1)} %fusion.104), channel_id=1, source_target_pairs={{0,1},{1,0},{2,3},{3,2},{4,5},{5,4},{6,7},{7,6},{8,9},{9,8},{10,11... | collective-permute-start | bytes 1179656 | tf_op jit(solution)/shard_map/ppermute | solution.py:386
  313.8 16.3 %collective-permute-start.31 = (bf16[256,768]{0,1:T(8,128)(2,1)}, bf16[256,768]{0,1:T(8,128)(2,1)}, u32[]{:S(2)}, u32[]{:S(2)}) collective-permute-start(bf16[256,768]{0,1:T(8,128)(2,1)} %copy.175), channel_id=1, source_target_pairs={{0,1},{1,0},{2,3},{3,2},{4,5},{5,4},{6,7},{7,6},{8,9},{9,8},{10,11... | collective-permute-start | bytes 1179656 | tf_op jit(solution)/shard_map/ppermute | solution.py:386
  338.0 202.0 %reduce-scatter.3.cloned.1.call-start = ((), (), s32[]{:S(2)}) async-start(), calls=%async_computation.2 | async-start | bytes 2654208 | tf_op jit(solution)/shard_map/reduce_scatter | solution.py:518
  387.1 18.1 %collective-permute-start.35 = (bf16[256,768]{0,1:T(8,128)(2,1)S(1)}, bf16[256,768]{0,1:T(8,128)(2,1)S(1)}, u32[]{:S(2)}, u32[]{:S(2)}) collective-permute-start(bf16[256,768]{0,1:T(8,128)(2,1)S(1)} %add_convert_fusion.3), channel_id=1, source_target_pairs={{0,2},{1,3},{2,0},{3,1},{4,6},{5,7},{6,4},{7,5},{8,10},{9,11},{10,... | collective-permute-start | bytes 1179656 | tf_op jit(solution)/shard_map/ppermute | solution.py:386
  409.6 40.3 %collective-permute-start.36 = (bf16[384,1536]{1,0:T(8,128)(2,1)}, bf16[384,1536]{1,0:T(8,128)(2,1)}, u32[]{:S(2)}, u32[]{:S(2)}) collective-permute-start(bf16[384,1536]{1,0:T(8,128)(2,1)} %get-tuple-element.123), channel_id=1, source_target_pairs={{0,1},{1,0},{2,3},{3,2},{4,5},{5,4},{6,7},{7,6},{8,9},{9,8},{10,11... | collective-permute-start | bytes 3538952 | tf_op jit(solution)/shard_map/ppermute | solution.py:386
  414.1 23.0 %collective-permute-start.58 = (f32[8,768]{1,0:T(8,128)S(1)}, f32[8,768]{1,0:T(8,128)S(1)}, u32[]{:S(2)}, u32[]{:S(2)}) collective-permute-start(f32[8,768]{1,0:T(8,128)S(1)} %add.310), channel_id=1, source_target_pairs={{0,4},{4,0},{8,12},{12,8},{16,20},{20,16},{24,28},{28,24},{1,5},{5... | collective-permute-start | bytes 73736 | tf_op jit(solution)/shard_map/ppermute | solution.py:386
  437.1 16.0 %collective-permute-start.46 = (bf16[384,1536]{1,0:T(8,128)(2,1)}, bf16[384,1536]{1,0:T(8,128)(2,1)}, u32[]{:S(2)}, u32[]{:S(2)}) collective-permute-start(bf16[384,1536]{1,0:T(8,128)(2,1)} %get-tuple-element.125), channel_id=1, source_target_pairs={{0,1},{1,0},{2,3},{3,2},{4,5},{5,4},{6,7},{7,6},{8,9},{9,8},{10,11... | collective-permute-start | bytes 3538952 | tf_op jit(solution)/shard_map/ppermute | solution.py:386
  451.7 15.3 %collective-permute-start.37 = (bf16[192,1536]{1,0:T(8,128)(2,1)S(1)}, bf16[192,1536]{1,0:T(8,128)(2,1)S(1)}, u32[]{:S(2)}, u32[]{:S(2)}) collective-permute-start(bf16[192,1536]{1,0:T(8,128)(2,1)S(1)} %dynamic-slice_bitcast_fusion.1), channel_id=1, source_target_pairs={{0,2},{1,3},{2,0},{3,1},{4,6},{5,7},{6,4},{7,5},{8,10},{9,11},{10,... | collective-permute-start | bytes 1769480 | tf_op jit(solution)/shard_map/ppermute | solution.py:386
  454.7 19.5 %collective-permute-start.47 = (bf16[192,1536]{1,0:T(8,128)(2,1)S(1)}, bf16[192,1536]{1,0:T(8,128)(2,1)S(1)}, u32[]{:S(2)}, u32[]{:S(2)}) collective-permute-start(bf16[192,1536]{1,0:T(8,128)(2,1)S(1)} %dynamic-slice_bitcast_fusion), channel_id=1, source_target_pairs={{0,4},{4,0},{8,12},{12,8},{16,20},{20,16},{24,28},{28,24},{1,5},{5... | collective-permute-start | bytes 1769480 | tf_op jit(solution)/shard_map/ppermute | solution.py:386
  481.3 13.2 %collective-permute-start.49 = (bf16[48,1536]{1,0:T(8,128)(2,1)S(1)}, bf16[48,1536]{1,0:T(8,128)(2,1)S(1)}, u32[]{:S(2)}, u32[]{:S(2)}) collective-permute-start(bf16[48,1536]{1,0:T(8,128)(2,1)S(1)} %dynamic-slice_bitcast_fusion.4), channel_id=1, source_target_pairs={{0,8},{4,12},{8,0},{12,4},{16,24},{20,28},{24,16},{28,20},{1,9},{5... | collective-permute-start | bytes 442376 | tf_op jit(solution)/shard_map/ppermute | solution.py:386
  519.1 15.9 %collective-permute-start.44 = (bf16[192,1536]{1,0:T(8,128)(2,1)S(1)}, bf16[192,1536]{1,0:T(8,128)(2,1)S(1)}, u32[]{:S(2)}, u32[]{:S(2)}) collective-permute-start(bf16[192,1536]{1,0:T(8,128)(2,1)S(1)} %pad_maximum_fusion.4), channel_id=1, source_target_pairs={{0,2},{1,3},{2,0},{3,1},{4,6},{5,7},{6,4},{7,5},{8,10},{9,11},{10,... | collective-permute-start | bytes 1769480 | tf_op jit(solution)/shard_map/ppermute | solution.py:386
  (96 other events, 805.2 us)
Sparse Core Ops, SparseCore 0:
  267.7 159.8 all-reduce.6
Sparse Core Ops, SparseCore 1:
  338.0 77.2 reduce-scatter.4
  419.1 79.8 reduce-scatter.2
where the time goes:
time: 569 us; the launch traced here: 560 us
  waiting for transfers between devices  187 us (33%)
  Pallas kernels  181 us (32%)
  local copies, waits for them, and re-layouts  80.3 us (14%)
  other arithmetic  42.5 us (7%)
  starting transfers between devices  38.4 us (7%)
  between operations  16.9 us (3%)
  matrix products  13.2 us (2%)
    ppermute x61, waiting for transfers between devices, swap(): return lax.ppermute(value, axis, [(i, i ^ bit) for i in range(size)])  177 us
    pallas_call x2, Pallas kernels, attn_bwd(): pl.pallas_call(functools.partial(attn_bwd_body, heads, blocks, layer), gr...  71.2 us
    pallas_call x2, Pallas kernels, attn_fwd(): pl.pallas_call(functools.partial(attn_fwd_body, blocks, heads, layer), gr...  54.1 us
    ppermute x61, starting transfers between devices, swap(): return lax.ppermute(value, axis, [(i, i ^ bit) for i in range(size)])  37.7 us
    pallas_call x2, Pallas kernels, expand(): pl.pallas_call(expand_body, grid=(steps,), in_specs=in_specs, out_specs=[...  18.9 us
    pallas_call x4, Pallas kernels, ffn_bwd(): pl.pallas_call(functools.partial(ffn_bwd_body, blocks), grid=(1,), in_spe...  18.8 us
    pallas_call x4, Pallas kernels, ffn_fwd(): pl.pallas_call(functools.partial(ffn_fwd_body, blocks), grid=(1,), in_spe...  18.3 us
    ppermute x12, local copies, waits for them, and re-layouts, swap(): return lax.ppermute(value, axis, [(i, i ^ bit) for i in range(size)])  15.1 us
  transfers between devices with their start and end apart: 64, of which 31 were waited for; matrix products, arithmetic and copies ran while one was open for 22% of the time, Pallas kernels for 15%

commit v1 on v0

--- a/solution.py
+++ b/solution.py
@@ -53,7 +53,7 @@
 def attn_fwd_body(blocks, heads, layer, *refs):
     n_refs = refs[:blocks]
     x_ref, wqkv_ref, wout_ref, tab_ref, gain_ref, qinfo_ref, kinfo_ref = refs[blocks : blocks + 7]
-    p_ref, u_ref, q_ref, k_ref, v_ref, o_ref, xm_ref, n2_ref, bias_ref, acc_ref = refs[blocks + 7 :]
+    p_ref, u_ref, q_ref, k_ref, v_ref, ot_ref, n1t_ref, xm_ref, n2_ref, bias_ref, acc_ref = refs[blocks + 7 :]
     step = pl.program_id(0)
     rows, width = x_ref.shape
 
@@ -83,7 +83,9 @@
     @pl.when(step == pl.num_programs(0) - 1)
     def _():
         o = acc_ref[...].astype(BF16)
-        o_ref[...] = o
+        ot_ref[...] = o.T
+        for r in range(blocks):
+            n1t_ref[:, r * rows : (r + 1) * rows] = n_refs[r][...].T
         xm = x_ref[...] + dot_nn(o, wout_ref[0])
         xm_ref[...] = xm
         n2_ref[...] = rms(xm, gain_ref[pl.ds(layer, 1), :]).astype(BF16)
@@ -105,7 +107,8 @@
         ((rows, width), BF16),
         ((keys, width), BF16),
         ((keys, width), BF16),
-        ((rows, width), BF16),
+        ((width, rows), BF16),
+        ((width, keys), BF16),
         ((rows, width), F32),
         ((rows, width), BF16),
     ]
@@ -271,33 +274,65 @@
         write(am_ref, bm_ref)
 
 
-def expand(layer, a_mine, a_other, b_mine, b_other, which, before=None):
-    half, width2 = a_mine.shape
-    width = width2 // 2
+def expand_first_body(both_ref, qkv_ref, out_ref):
+    width = out_ref.shape[2]
+    qkv_ref[0, :, : 2 * width] = both_ref[:, 2 * width :].astype(F32)
+    qkv_ref[0, :, 2 * width :] = both_ref[:, :width].astype(F32)
+    out_ref[0] = both_ref[:, width : 2 * width].astype(F32)
+
+
+def expand_first(layer, both):
+    rows, width4 = both.shape
+    width = width4 // 4
     steps = 8
-    per = 2 * half // steps
-    block = pl.BlockSpec((per, width2), lambda i: (i % (steps // 2), 0))
-    in_specs = [pl.BlockSpec(memory_space=pltpu.SMEM)] + [block] * 4
-    args = [which, a_mine, a_other, b_mine, b_other]
-    aliases = {}
-    if before is not None:
-        in_specs += [pl.BlockSpec(memory_space=pl.ANY)] * 2
-        args += before
-        aliases = {5: 0, 6: 1}
+    per = rows // steps
     return pl.pallas_call(
-        expand_body,
+        expand_first_body,
         grid=(steps,),
-        in_specs=in_specs,
+        in_specs=[pl.BlockSpec((per, width4), lambda i: (i, 0))],
         out_specs=[
             pl.BlockSpec((1, per, 3 * width), lambda i: (layer, i, 0)),
             pl.BlockSpec((1, per, width), lambda i: (layer, i, 0)),
         ],
         out_shape=[
+            jax.ShapeDtypeStruct((LAYERS, rows, 3 * width), F32),
+            jax.ShapeDtypeStruct((LAYERS, rows, width), F32),
+        ],
+        compiler_params=pltpu.CompilerParams(vmem_limit_bytes=VMEM),
+        cost_estimate=pl.CostEstimate(flops=0, bytes_accessed=14_000_000, transcendentals=0),
+        name="expand_first",
+    )(both)
+
+
+def expand(layer, a_mine, a_other, b_mine, b_other, which, before):
+    half, width2 = a_mine.shape
+    width = width2 // 2
+    steps = 8
+    each = steps // 2
+    per = half // each
+    mine = pl.BlockSpec((per, width2), lambda i, w: (jnp.clip(i - each * w[0], 0, each - 1), 0))
+    other = pl.BlockSpec((per, width2), lambda i, w: (jnp.clip(i - each * (1 - w[0]), 0, each - 1), 0))
+    in_specs = [mine, other, mine, other]
+    args = [which, a_mine, a_other, b_mine, b_other, *before]
+    in_specs += [pl.BlockSpec(memory_space=pl.ANY)] * 2
+    return pl.pallas_call(
+        expand_body,
+        grid_spec=pltpu.PrefetchScalarGridSpec(
+            num_scalar_prefetch=1,
+            grid=(steps,),
+            in_specs=in_specs,
+            out_specs=[
+                pl.BlockSpec((1, per, 3 * width), lambda i, w: (layer, i, 0)),
+                pl.BlockSpec((1, per, width), lambda i, w: (layer, i, 0)),
+            ],
+        ),
+        out_shape=[
             jax.ShapeDtypeStruct((LAYERS, 2 * half, 3 * width), F32),
             jax.ShapeDtypeStruct((LAYERS, 2 * half, width), F32),
         ],
-        input_output_aliases=aliases,
-        cost_estimate=pl.CostEstimate(flops=0, bytes_accessed=20_000_000, transcendentals=0),
+        input_output_aliases={5: 0, 6: 1},
+        compiler_params=pltpu.CompilerParams(vmem_limit_bytes=VMEM),
+        cost_estimate=pl.CostEstimate(flops=0, bytes_accessed=14_000_000, transcendentals=0),
         name="expand",
     )(*args)
 
@@ -381,41 +416,122 @@
     return res[:blocks], res[blocks]
 
 
+def ffn_grads_body(blocks, chunks, *refs):
+    n_refs, g_refs = refs[:blocks], refs[blocks : 2 * blocks]
+    hid_refs, gpre_refs = refs[2 * blocks : 2 * blocks + 2], refs[2 * blocks + 2 : 2 * blocks + 4]
+    out_ref = refs[-1]
+    rows, width = n_refs[0].shape
+    per = width // chunks
+    for part, (left_refs, right_refs) in enumerate(((n_refs, gpre_refs), (g_refs, hid_refs))):
+        left = jnp.concatenate([ref[...].T for ref in left_refs], 1)
+        right = jnp.concatenate([ref[...] for ref in right_refs], 0)
+        grad = dot_nn(left, right).astype(BF16)
+        for c in range(chunks):
+            place = 2 * sum(((c >> i) & 1) * (chunks >> (i + 1)) for i in range(chunks.bit_length() - 1)) + part
+            out_ref[place * per : (place + 1) * per, :] = grad[c * per : (c + 1) * per]
+
+
+def ffn_grads(n_blocks, g_blocks, hids, gpres, chunks):
+    blocks = len(n_blocks)
+    rows, width = n_blocks[0].shape
+    hidden = hids[0].shape[1]
+    args = (*n_blocks, *g_blocks, *hids, *gpres)
+    return pl.pallas_call(
+        functools.partial(ffn_grads_body, blocks, chunks),
+        grid=(1,),
+        in_specs=[whole(a.shape) for a in args],
+        out_specs=whole((2 * width, hidden)),
+        out_shape=jax.ShapeDtypeStruct((2 * width, hidden), BF16),
+        compiler_params=pltpu.CompilerParams(vmem_limit_bytes=VMEM),
+        cost_estimate=pl.CostEstimate(
+            flops=4 * rows * blocks * width * hidden, bytes_accessed=9_000_000, transcendentals=0
+        ),
+        name="ffn_grads",
+    )(*args)
+
+
 def swap(value, axis, bit):
     size = lax.axis_size(axis)
     return lax.ppermute(value, axis, [(i, i ^ bit) for i in range(size)])
 
 
+def after(values, *done):
+    return lax.optimization_barrier((values, done))[0]
+
+
+def gather_near(value):
+    half = lax.axis_size("tp") // 2
+    far = swap(value, "tp", half)
+    near = [value]
+    bit = 1
+    while bit < half:
+        near += [swap(b, "tp", bit) for b in near]
+        bit *= 2
+    return near, far
+
+
+def gather_far(far):
+    half = lax.axis_size("tp") // 2
+    blocks = [far]
+    bit = 1
+    while bit < half:
+        blocks += [swap(b, "tp", bit) for b in blocks]
+        bit *= 2
+    return blocks
+
+
 def gather_blocks(value):
-    blocks = {0: value}
-    bit = lax.axis_size("tp") // 2
-    while bit:
-        for r in list(blocks):
-            blocks[r | bit] = swap(blocks[r], "tp", bit)
-        bit //= 2
-    return [blocks[r] for r in range(len(blocks))]
-
-
-def scatter_sum(blocks):
+    near, far = gather_near(value)
+    return near + gather_far(far)
+
+
+def scatter_begin(blocks):
     blocks = list(blocks)
     bit = 1
-    while bit < lax.axis_size("tp"):
+    while bit < lax.axis_size("tp") // 2:
         size = len(blocks)
         keep = [blocks[r] for r in range(size) if not r & 1]
         sent = [swap(blocks[r], "tp", bit) for r in range(size) if r & 1]
         blocks = [a.astype(F32) + b.astype(F32) for a, b in zip(keep, sent)]
         bit *= 2
-        if bit < lax.axis_size("tp"):
-            blocks = [blocks[0]] + [b.astype(BF16) for b in blocks[1:]]
-    return blocks[0]
-
-
-def halve(part, axis, bit):
+        blocks = [blocks[0]] + [b.astype(BF16) for b in blocks[1:]]
+    return blocks[0].astype(F32), swap(blocks[1], "tp", bit)
+
+
+def halve_begin(part, axis, bit):
     mine = (lax.axis_index(axis) // bit) & 1
     pair = part.reshape(2, part.shape[0] // 2, part.shape[1])
     sent = lax.dynamic_index_in_dim(pair, 1 - mine, 0, keepdims=False)
     kept = lax.dynamic_index_in_dim(pair, mine, 0, keepdims=False)
-    return (kept.astype(F32) + swap(sent, axis, bit).astype(F32)).astype(BF16)
+    return kept, swap(sent, axis, bit)
+
+
+def halve_end(kept, got):
+    return (kept.astype(F32) + got.astype(F32)).astype(BF16)
+
+
+class Scatter:
+    def __init__(self, parts, steps):
+        self.steps = list(steps)
+        self.begin(parts)
+
+    def begin(self, parts):
+        step = self.steps.pop(0)
+        self.kept, self.got = zip(*[halve_begin(part, *step) for part in parts])
+
+    def advance(self, *done):
+        if self.steps:
+            got = after(self.got, *done)
+            self.begin([halve_end(a, b) for a, b in zip(self.kept, got)])
+
+    def finish(self, *done):
+        while self.steps:
+            self.advance(*done)
+        return [a.astype(F32) + b.astype(F32) for a, b in zip(self.kept, after(self.got, *done))]
+
+
+def halve(part, axis, bit):
+    return halve_end(*halve_begin(part, axis, bit))
 
 
 def double(part, axis, bit):
@@ -428,20 +544,39 @@
     return [(axis, 1 << i) for i in range(lax.axis_size(axis).bit_length() - 1)]
 
 
-def sum_halves(keep_a, send_a, keep_b, send_b):
+def sum_orders():
     first, *tp_rest = steps_of("tp")
     dp_first, *dp_rest = steps_of("dp")
-    orders = (tp_rest + [dp_first] + dp_rest, [dp_first] + tp_rest + dp_rest)
-    parts = [
-        (keep.astype(F32) + swap(send, *first).astype(F32)).astype(BF16)
-        for keep, send in ((keep_a, send_a), (keep_b, send_b))
-    ]
-    for stage in range(len(orders[0])):
+    return first, (tp_rest + [dp_first] + dp_rest, [dp_first] + tp_rest + dp_rest)
+
+
+def sum_begin(keep_a, send_a, keep_b, send_b):
+    first, _ = sum_orders()
+    return [halve_end(keep, swap(send, *first)) for keep, send in ((keep_a, send_a), (keep_b, send_b))]
+
+
+def sum_middle(parts, first_stage, last_stage=None):
+    _, orders = sum_orders()
+    for stage in range(len(orders[0]))[first_stage:last_stage]:
         parts = [halve(part, *order[stage]) for part, order in zip(parts, orders)]
+    return parts
+
+
+def sum_end(parts):
+    first, orders = sum_orders()
     for stage in range(len(orders[0]) - 1, -1, -1):
         parts = [double(part, *order[stage]) for part, order in zip(parts, orders)]
     others = [swap(part, *first) for part in parts]
     return parts[0], others[0], parts[1], others[1]
+
+
+def gather_all(pieces, order):
+    both = lax.all_gather(jnp.concatenate(pieces, 1), ("dp", "tp"))
+    bits = len(order)
+    names = steps_of("dp")[::-1] + steps_of("tp")[::-1]
+    both = both.reshape((2,) * bits + both.shape[1:])
+    both = both.transpose([names.index(step) for step in order] + [bits, bits + 1])
+    return both.reshape(-1, both.shape[-1])
 
 
 def butterfly(value):
@@ -473,12 +608,15 @@
     tabt = jnp.pad(jnp.repeat(jnp.swapaxes(tab, 1, 2), head_size, axis=1), ((0, 0), (0, 0), (0, 128 - 2 * heads)))
     tab = jnp.repeat(tab, head_size, axis=2)
 
-    grad_last = gather_blocks(cotangent[:, 0])
     stream = x_in[:, 0].astype(F32)
     kept = []
+    half = tp_size // 2
     for layer in range(LAYERS):
+        last = layer == LAYERS - 1
         n1_blocks = gather_blocks(rms(stream, gain_attn[layer]).astype(BF16))
-        p, u, q, k, v, o, middle, n2 = attn_fwd(
+        if last:
+            grad_near, grad_far = gather_near(after(cotangent[:, 0], n1_blocks[half]))
+        p, u, q, k, v, ot, n1t, middle, n2 = attn_fwd(
             layer,
             n1_blocks,
             stream,
@@ -488,65 +626,81 @@
             gain_ffn,
             where,
         )
-        n2_blocks = gather_blocks(n2)
-        half = tp_size // 2
-        out_a, hid_a, dgelu_a = ffn_fwd(layer, n2_blocks[:half], w_in, w_down)
+        if last:
+            n2, grad_near, grad_far = after((n2, grad_near, grad_far))
+        near, far = gather_near(n2)
+        out_a, hid_a, dgelu_a = ffn_fwd(layer, near, w_in, w_down)
+        if last:
+            gn2_a, gpre_a = ffn_bwd(layer, grad_near, dgelu_a, w_in, w_down)
+            far = after(far, gpre_a)
+            gf_blocks = grad_near + gather_far(grad_far)
+        n2_blocks = near + gather_far(after(far, hid_a))
         out_b, hid_b, dgelu_b = ffn_fwd(layer, n2_blocks[half:], w_in, w_down)
-        kept.append((stream, n1_blocks, p, u, q, k, v, o, middle, n2_blocks, hid_a, hid_b, dgelu_a, dgelu_b))
-        stream = middle + scatter_sum([*out_a, *out_b])
-    y_out = stream.astype(BF16)
+        kept.append((stream, n1t, p, u, q, k, v, ot, middle, n2_blocks, hid_a, hid_b, dgelu_a, dgelu_b))
+        if not last:
+            own, far = scatter_begin([*out_a, *out_b])
+            stream = middle + (own + far.astype(F32))
 
     grad_flow = cotangent[:, 0].astype(F32)
+    per = width // dp_size
     small = [None] * LAYERS
-    replicated = None
     sharded = [None] * LAYERS
     for layer in range(LAYERS - 1, -1, -1):
-        stream, n1_blocks, p, u, q, k, v, o, middle, n2_blocks, hid_a, hid_b, dgelu_a, dgelu_b = kept[layer]
-        gf_blocks = grad_last if layer == LAYERS - 1 else gather_blocks(grad_flow.astype(BF16))
-        gn2_a, gpre_a = ffn_bwd(layer, gf_blocks[:half], dgelu_a, w_in, w_down)
+        last = layer == LAYERS - 1
+        stream, n1t, p, u, q, k, v, ot, middle, n2_blocks, hid_a, hid_b, dgelu_a, dgelu_b = kept[layer]
+        if not last:
+            near, far = gather_near(grad_flow.astype(BF16))
+            gn2_a, gpre_a = ffn_bwd(layer, near, dgelu_a, w_in, w_down)
+            gf_blocks = near + gather_far(after(far, gpre_a))
         gn2_b, gpre_b = ffn_bwd(layer, gf_blocks[half:], dgelu_b, w_in, w_down)
-        gf_all = jnp.concatenate(gf_blocks, 0)
-        n2_all = jnp.concatenate(n2_blocks, 0)
-        gpre = jnp.concatenate([gpre_a, gpre_b], 0)
-        hid = jnp.concatenate([hid_a, hid_b], 0)
-        grad_win = dot_tn(n2_all, gpre).astype(BF16)
-        grad_wdown_t = dot_tn(gf_all, hid).astype(BF16)
-        per = width // dp_size
-        packed = jnp.concatenate(
-            [grad_win.reshape(dp_size, per, -1), grad_wdown_t.reshape(dp_size, per, -1)], 1
-        ).reshape(2 * width, -1)
-        summed = lax.psum_scatter(packed, "dp", scatter_dimension=0, tiled=True).astype(F32)
-        sharded[layer] = (summed[:per], summed[per:].T)
-
-        gn2 = scatter_sum([*gn2_a, *gn2_b]).astype(BF16).astype(F32)
+        if not last:
+            moving.advance(gpre_b)
+            summing.advance(gpre_b)
+        own, far = scatter_begin([*gn2_a, *gn2_b])
+        packed = ffn_grads(n2_blocks, gf_blocks, (hid_a, hid_b), (gpre_a, gpre_b), dp_size)
+        far, packed = after((far, packed))
+        if not last:
+            (summed,) = moving.finish(packed)
+            sharded[layer + 1] = (summed[:per], summed[per:].T)
+            summing.advance(packed)
+        moving = Scatter([packed], steps_of("dp"))
+        if last:
+            own_y, far_y = scatter_begin(after([*out_a, *out_b], packed))
+        gn2 = (own + far.astype(F32)).astype(BF16).astype(F32)
         grad_norm, grad_gffn = rms_back(gn2, middle, gain_ffn[layer])
         grad_middle = grad_flow + grad_norm
         ga = grad_middle.astype(BF16)
-        core = tp_index & 1 if layer == 0 else jnp.int32(0)
+        core = (tp_index & 1)[None]
         parts, grads, zpre, zpost = attn_bwd(
-            layer,
-            tp_size,
-            ga,
-            w_out,
-            q,
-            k,
-            v,
-            p,
-            u,
-            tab,
-            tabt,
-            core[None],
-            w_qkv,
-            jnp.concatenate(n1_blocks, 0).T,
-            o.T,
+            layer, tp_size, ga, w_out, q, k, v, p, u, tab, tabt, core, w_qkv, n1t, ot
         )
-        if layer == 0:
-            keep_a, send_a, keep_b, send_b = grads
-            replicated = expand(layer, *sum_halves(keep_a, send_a, keep_b, send_b), core[None], replicated)
+        if last:
+            parts, grads, moving.got, far_y = after((parts, grads, moving.got, far_y))
+            y_out = (middle + (own_y + far_y.astype(F32))).astype(BF16)
         else:
-            keep_a, send_a, keep_b, send_b = lax.psum(tuple(grads), ("dp", "tp"))
-            replicated = expand(layer, keep_a, send_a, keep_b, send_b, core[None], replicated)
-        gn1 = scatter_sum(parts).astype(BF16).astype(F32)
+            parts, grads, moving.got, summing.got = after((parts, grads, moving.got, summing.got))
+        pieces = sum_begin(*grads)
+        own, far = scatter_begin(parts)
+        if last:
+            moving.advance()
+            far = after(far, *pieces)
+            order = steps_of("dp") + steps_of("tp")[1:]
+            summing = Scatter(pieces, order)
+        else:
+            reduced = summing.finish()
+            pieces = sum_middle(pieces, 0, 1)
+            far = after(far, *pieces)
+            moving.advance(*pieces)
+            reduced = after([r.astype(BF16) for r in reduced], *pieces)
+            gathered = gather_all(reduced, steps_of("tp")[:1] + order)
+            pieces = sum_middle(pieces, 1)
+            late = pieces
+            moving.advance(*pieces)
+            pieces = sum_end(pieces)
+            replicated = expand(0, *pieces, core, expand_first(1, gathered))
+            (summed,) = moving.finish()
+            sharded[layer] = (summed[:per], summed[per:].T)
+        gn1 = (own + far.astype(F32)).astype(BF16).astype(F32)
         grad_norm, grad_gattn = rms_back(gn1, stream, gain_attn[layer])
         grad_flow = grad_middle + grad_norm
         grad_mpre = jnp.sum(zpre.reshape(heads, heads, head_size), -1).T * (head_size**-0.5)
@@ -561,7 +715,7 @@
         + [g[None] for s in small for g in s[2:]]
     )
     flat = jnp.pad(flat, ((0, -flat.shape[0] % 8), (0, 0)))
-    flat = butterfly(flat)
+    flat = butterfly(after(flat, *late))
     mixes = flat[:mix_rows].reshape(-1)[:count].reshape(LAYERS, 2, heads, heads)
     gains = flat[mix_rows : mix_rows + 2 * LAYERS].reshape(LAYERS, 2, width)
     return (

time: 569 us -> 507 us (0.89)
  waiting for transfers between devices: 187 us -> 141 us
  local copies, waits for them, and re-layouts: 80.3 us -> 43 us
  starting transfers between devices: 38.4 us -> 61.7 us
  matrix products: 13.2 us -> 0 us
  Pallas kernels: 181 us -> 193 us
    ppermute x61 -> x77, waiting for transfers between devices: 177 us -> 141 us  [swap(): return lax.ppermute(value, axis, [(i, i ^ bit) for i in range(size)])]
    pallas_call x24 -> x0, local copies, waits for them, and re-layouts: 31.8 us -> none  [the longest x8 14.8 us: ffn_bwd(): pl.pallas_call(functools.partial(ffn_bwd_body, blocks), grid=(1,), in_spe...]
    ppermute x61 -> x77, starting transfers between devices: 37.7 us -> 61.7 us  [swap(): return lax.ppermute(value, axis, [(i, i ^ bit) for i in range(size)])]
    ppermute x12 -> x0, local copies, waits for them, and re-layouts: 15.1 us -> none  [swap(): return lax.ppermute(value, axis, [(i, i ^ bit) for i in range(size)])]
    dot_general x4 -> x0, matrix products: 13.2 us -> none  [dot_tn(): lax.dot_general(a, b, (((0,), (0,)), ((), ())), preferred_element_type=F32)]
    squeeze x8 -> x22, local copies, waits for them, and re-layouts: 0.23 us -> 12.8 us  [halve_begin(): sent = lax.dynamic_index_in_dim(pair, 1 - mine, 0, keepdims=False)]
    psum x1 -> x0, waiting for transfers between devices: 10.4 us -> none  [on_device(): keep_a, send_a, keep_b, send_b = lax.psum(tuple(grads), ('dp', 'tp'))]
    pallas_call x2 -> x4, Pallas kernels: 18.9 us -> 29.2 us  [the longest x2 13.7 us: ffn_grads(): pl.pallas_call(functools.partial(ffn_grads_body, blocks, chunks), grid=(1...]
  transfers between devices with their start and end apart: 64 -> 78, of which waited for: 31 -> 33; matrix products, arithmetic and copies ran while one was open for 22% -> 15% of each run, Pallas kernels for 15% -> 30%
where the time goes in v1:
time: 507 us; the launch traced here: 498 us
  Pallas kernels  193 us (38%)
  waiting for transfers between devices  141 us (28%)
  starting transfers between devices  61.7 us (12%)
  local copies, waits for them, and re-layouts  43 us (8%)
  other arithmetic  43 us (8%)
  between operations  15.9 us (3%)
    ppermute x77, waiting for transfers between devices, swap(): return lax.ppermute(value, axis, [(i, i ^ bit) for i in range(size)])  141 us
    pallas_call x2, Pallas kernels, attn_bwd(): pl.pallas_call(functools.partial(attn_bwd_body, heads, blocks, layer), gr...  71.8 us
    ppermute x77, starting transfers between devices, swap(): return lax.ppermute(value, axis, [(i, i ^ bit) for i in range(size)])  61.7 us
    pallas_call x2, Pallas kernels, attn_fwd(): pl.pallas_call(functools.partial(attn_fwd_body, blocks, heads, layer), gr...  55.1 us
    convert_element_type x22, other arithmetic, halve_end(): return (kept.astype(F32) + got.astype(F32)).astype(BF16)  20.4 us
    pallas_call x4, Pallas kernels, ffn_bwd(): pl.pallas_call(functools.partial(ffn_bwd_body, blocks), grid=(1,), in_spe...  18.8 us
    pallas_call x4, Pallas kernels, ffn_fwd(): pl.pallas_call(functools.partial(ffn_fwd_body, blocks), grid=(1,), in_spe...  18.3 us
    pallas_call x2, Pallas kernels, ffn_grads(): pl.pallas_call(functools.partial(ffn_grads_body, blocks, chunks), grid=(1...  13.7 us
  transfers between devices with their start and end apart: 78, of which 33 were waited for; matrix products, arithmetic and copies ran while one was open for 15% of the time, Pallas kernels for 30%

profile of v1, /device:TPU:0, one launch (start us, length us, event | category | flops | bytes accessed | tf_op | source)
XLA Modules:
  0.0 497.6 jit_solution(4203081947582557267)
XLA Ops:
  13.7 8.9 %collective-permute-done.1.refs_2_ = bf16[256,768]{1,0:T(8,128)(2,1)S(1)} collective-permute-done((bf16[256,768]{1,0:T(8,128)(2,1)S(1)}, bf16[256,768]{1,0:T(8,128)(2,1)S(1)}, u32[]{:S(2)}, u32[]{:S(2)}) %collective-permute-start.1) | collective-permute-done | bytes 393248 | tf_op jit(solution)/shard_map/ppermute | solution.py:455
  27.4 27.4 %attn_fwd.2 = (bf16[12,256,1024]{2,1,0:T(8,128)(2,1)}, bf16[12,256,768]{2,1,0:T(8,128)(2,1)}, bf16[256,768]{1,0:T(8,128)(2,1)}, bf16[1024,768]{1,0:T(8,128)(2,1)...) custom-call(bf16[256,768]{1,0:T(8,128)(2,1)} %copy-done.36, ...), custom_call_target="tpu_custom_call" | custom-call | flops 9663676416 | bytes 20000000 | tf_op jit(solution)/shard_map/attn_fwd/pallas_call | solution.py:118
  78.6 9.4 %collective-permute-done.8 = bf16[256,768]{1,0:T(8,128)(2,1)S(1)} collective-permute-done((bf16[256,768]{1,0:T(8,128)(2,1)S(1)}, bf16[256,768]{1,0:T(8,128)(2,1)S(1)}, u32[]{:S(2)}, u32[]{:S(2)}) %collective-permute-start.8) | collective-permute-done | bytes 393248 | tf_op jit(solution)/shard_map/ppermute | solution.py:455
  90.9 8.6 %collective-permute-done.10.refs_2_ = bf16[256,768]{1,0:T(8,128)(2,1)S(1)} collective-permute-done((bf16[256,768]{1,0:T(8,128)(2,1)S(1)}, bf16[256,768]{1,0:T(8,128)(2,1)S(1)}, u32[]{:S(2)}, u32[]{:S(2)}) %collective-permute-start.10) | collective-permute-done | bytes 393248 | tf_op jit(solution)/shard_map/ppermute | solution.py:455
  102.5 27.7 %attn_fwd.3 = (bf16[12,256,1024]{2,1,0:T(8,128)(2,1)}, bf16[12,256,768]{2,1,0:T(8,128)(2,1)}, bf16[256,768]{1,0:T(8,128)(2,1)}, bf16[1024,768]{1,0:T(8,128)(2,1)...) custom-call(bf16[256,768]{1,0:T(8,128)(2,1)} %copy-done.42, ...), custom_call_target="tpu_custom_call" | custom-call | flops 9663676416 | bytes 20000000 | tf_op jit(solution)/shard_map/attn_fwd/pallas_call | solution.py:118
  133.0 4.6 ffn_fwd.6
  137.6 4.7 ffn_bwd.4
  150.1 4.7 ffn_bwd.5
  158.1 6.8 %ffn_grads.2 = bf16[1536,768]{1,0:T(8,128)(2,1)} custom-call(bf16[256,768]{1,0:T(8,128)(2,1)} %get-tuple-element.146.refs_0_, bf16[256,768]{1,0:T(8,128)(2,1)} %copy-done.50, bf16[256,768]{1,0:T(8,128)(2,1)} %copy-done.51, bf16[256,768]{1,0:T(8,128)(2,1)} %copy-done.52, bf16[256,768]{1,0:T(8,128)(2,1)} %bitcast.223, bf16[256,768]{1,0:T(8,128)(2,1)} %copy-done.32, ...), custom_call_target="tpu_custom_call" | custom-call | flops 2415919104 | bytes 9000000 | tf_op jit(solution)/shard_map/ffn_grads/pallas_call | solution.py:439
  174.8 35.9 %attn_bwd.2 = (bf16[256,768]{1,0:T(8,128)(2,1)}, bf16[256,768]{1,0:T(8,128)(2,1)}, bf16[256,768]{1,0:T(8,128)(2,1)}, bf16[256,768]{1,0:T(8,128)(2,1)}, bf16[384,...) custom-call(bf16[256,768]{1,0:T(8,128)(2,1)} %get-tuple-element.307., ...), custom_call_target="tpu_custom_call" | custom-call | flops 38654705664 | bytes 20000000 | tf_op jit(solution)/shard_map/attn_bwd/pallas_call | solution.py:229
  224.7 6.4 %collective-permute-done.27 = bf16[256,768]{1,0:T(8,128)(2,1)S(1)} collective-permute-done((bf16[256,768]{1,0:T(8,128)(2,1)S(1)}, bf16[256,768]{1,0:T(8,128)(2,1)S(1)}, u32[]{:S(2)}, u32[]{:S(2)}) %collective-permute-start.27) | collective-permute-done | bytes 393248 | tf_op jit(solution)/shard_map/ppermute | solution.py:455
  237.7 4.7 ffn_bwd.6
  250.7 4.7 ffn_bwd.7
  255.5 7.8 %collective-permute-done.37 = bf16[192,1536]{1,0:T(8,128)(2,1)} collective-permute-done((bf16[192,1536]{1,0:T(8,128)(2,1)}, bf16[192,1536]{1,0:T(8,128)(2,1)}, u32[]{:S(2)}, u32[]{:S(2)}) %collective-permute-start.37) | collective-permute-done | bytes 589856 | tf_op jit(solution)/shard_map/ppermute | solution.py:455
  276.3 6.8 %ffn_grads.3 = bf16[1536,768]{1,0:T(8,128)(2,1)} custom-call(bf16[256,768]{1,0:T(8,128)(2,1)} %get-tuple-element.136.refs_0_, bf16[256,768]{1,0:T(8,128)(2,1)} %copy-done.47, bf16[256,768]{1,0:T(8,128)(2,1)} %copy-done.48, bf16[256,768]{1,0:T(8,128)(2,1)} %copy-done.49, bf16[256,768]{1,0:T(8,128)(2,1)} %fusion.48.refs_0_.refs_4_, ...), custom_call_target="tpu_custom_call" | custom-call | flops 2415919104 | bytes 9000000 | tf_op jit(solution)/shard_map/ffn_grads/pallas_call | solution.py:439
  297.1 35.9 %attn_bwd.3 = (bf16[256,768]{1,0:T(8,128)(2,1)}, bf16[256,768]{1,0:T(8,128)(2,1)}, bf16[256,768]{1,0:T(8,128)(2,1)}, bf16[256,768]{1,0:T(8,128)(2,1)}, bf16[384,...) custom-call(bf16[256,768]{1,0:T(8,128)(2,1)} %get-tuple-element.303., ...), custom_call_target="tpu_custom_call" | custom-call | flops 38654705664 | bytes 20000000 | tf_op jit(solution)/shard_map/attn_bwd/pallas_call | solution.py:229
  349.4 10.8 %collective-permute-done.49 = bf16[192,1536]{1,0:T(8,128)(2,1)S(1)} collective-permute-done((bf16[192,1536]{1,0:T(8,128)(2,1)S(1)}, bf16[192,1536]{1,0:T(8,128)(2,1)S(1)}, u32[]{:S(2)}, u32[]{:S(2)}) %collective-permute-start.49) | collective-permute-done | bytes 589856 | tf_op jit(solution)/shard_map/ppermute | solution.py:455
  407.0 9.9 %collective-permute-done.61 = bf16[24,1536]{1,0:T(8,128)(2,1)S(1)} collective-permute-done((bf16[24,1536]{1,0:T(8,128)(2,1)S(1)}, bf16[24,1536]{1,0:T(8,128)(2,1)S(1)}, u32[]{:S(2)}, u32[]{:S(2)}) %collective-permute-start.61) | collective-permute-done | bytes 73760 | tf_op jit(solution)/shard_map/ppermute | solution.py:455
  421.6 6.2 %collective-permute-done.72 = f32[8,768]{1,0:T(8,128)S(1)} collective-permute-done((f32[8,768]{1,0:T(8,128)S(1)}, f32[8,768]{1,0:T(8,128)S(1)}, u32[]{:S(2)}, u32[]{:S(2)}) %collective-permute-start.72) | collective-permute-done | bytes 24608 | tf_op jit(solution)/shard_map/ppermute | solution.py:455
  427.9 5.9 %collective-permute-done.62 = bf16[48,1536]{1,0:T(8,128)(2,1)S(1)} collective-permute-done((bf16[48,1536]{1,0:T(8,128)(2,1)S(1)}, bf16[48,1536]{1,0:T(8,128)(2,1)S(1)}, u32[]{:S(2)}, u32[]{:S(2)}) %collective-permute-start.62) | collective-permute-done | bytes 147488 | tf_op jit(solution)/shard_map/ppermute | solution.py:455
  452.6 8.9 %collective-permute-done.64 = bf16[192,1536]{1,0:T(8,128)(2,1)S(1)} collective-permute-done((bf16[192,1536]{1,0:T(8,128)(2,1)S(1)}, bf16[192,1536]{1,0:T(8,128)(2,1)S(1)}, u32[]{:S(2)}, u32[]{:S(2)}) %collective-permute-start.64) | collective-permute-done | bytes 589856 | tf_op jit(solution)/shard_map/ppermute | solution.py:455
  469.7 5.0 %copy.43 = bf16[2,2,2,2,2,24,3072]{6,5,4,3,2,1,0:T(8,128)(2,1)} copy(bf16[2,2,2,2,2,24,3072]{6,5,0,4,1,2,3:T(8,128)(2,1)} %bitcast.200) | data formatting | bytes 9437184 | tf_op jit(solution)/shard_map/transpose | solution.py:578
  474.7 7.6 %expand_first.1 = (f32[2,768,2304]{2,1,0:T(8,128)}, f32[2,768,768]{2,1,0:T(8,128)}) custom-call(bf16[768,3072]{1,0:T(8,128)(2,1)} %bitcast.191), custom_call_target="tpu_custom_call" | custom-call | bytes 14000000 | tf_op jit(solution)/shard_map/expand_first/pallas_call | solution.py:289
  482.3 8.0 %expand.1 = (f32[2,768,2304]{2,1,0:T(8,128)}, f32[2,768,768]{2,1,0:T(8,128)}) custom-call(s32[1]{0:T(128)} %bitcast.13.refs_9_.refs_0_, bf16[384,1536]{1,0:T(8,128)(2,1)} %copy-done.6, bf16[384,1536]{1,0:T(8,128)(2,1)} %collective-permute-done.57.refs_2_, bf16[384,1536]{1,0:T(8,128)(2,1)} %copy-done.5, ...), custom_call_target="tpu_custom_call", output_to_operand_aliasing={{0}: (5, {}), {1}: (6, {})} | custom-call | bytes 14000000 | tf_op jit(solution)/shard_map/expand/pallas_call | solution.py:318
  (459 shorter events, 214.2 us)
Async XLA Ops:
  7.2 462.5 %all-gather.3.cloned.1.call-start = ((), (), s32[]{:S(2)}) async-start(), calls=%async_computation | async-start | bytes 4866048 | tf_op jit(solution)/shard_map/all_gather | solution.py:574
  99.5 30.7 %collective-permute-start.12 = (bf16[256,768]{1,0:T(8,128)(2,1)S(1)}, bf16[256,768]{1,0:T(8,128)(2,1)S(1)}, u32[]{:S(2)}, u32[]{:S(2)}) collective-permute-start(bf16[256,768]{1,0:T(8,128)(2,1)S(1)} %bitcast.224), channel_id=1, source_target_pairs={{0,1},{1,0},{2,3},{3,2},{4,5},{5,4},{6,7},{7,6},{8,9},{9,8},{10,11... | collective-permute-start | bytes 1179656 | tf_op jit(solution)/shard_map/ppermute | solution.py:455
  100.0 30.2 %collective-permute-start.13 = (bf16[256,768]{1,0:T(8,128)(2,1)S(1)}, bf16[256,768]{1,0:T(8,128)(2,1)S(1)}, u32[]{:S(2)}, u32[]{:S(2)}) collective-permute-start(bf16[256,768]{1,0:T(8,128)(2,1)S(1)} %bitcast.225), channel_id=1, source_target_pairs={{0,2},{1,3},{2,0},{3,1},{4,6},{5,7},{6,4},{7,5},{8,10},{9,11},{10,... | collective-permute-start | bytes 1179656 | tf_op jit(solution)/shard_map/ppermute | solution.py:455
  171.5 39.2 %collective-permute-start.22 = (bf16[768,768]{1,0:T(8,128)(2,1)}, bf16[768,768]{1,0:T(8,128)(2,1)}, u32[]{:S(2)}, u32[]{:S(2)}) collective-permute-start(bf16[768,768]{1,0:T(8,128)(2,1)} %dynamic-slice_bitcast_fusion.1), channel_id=1, source_target_pairs={{0,4},{4,0},{8,12},{12,8},{16,20},{20,16},{24,28},{28,24},{1,5},{5... | collective-permute-start | bytes 3538952 | tf_op jit(solution)/shard_map/ppermute | solution.py:455
  174.2 36.6 %collective-permute-start.24 = (bf16[256,768]{1,0:T(8,128)(2,1)S(1)}, bf16[256,768]{1,0:T(8,128)(2,1)}, u32[]{:S(2)}, u32[]{:S(2)}) collective-permute-start(bf16[256,768]{1,0:T(8,128)(2,1)S(1)} %add_convert_fusion.11), channel_id=1, source_target_pairs={{0,2},{1,3},{2,0},{3,1},{4,6},{5,7},{6,4},{7,5},{8,10},{9,11},{10,... | collective-permute-start | bytes 1179656 | tf_op jit(solution)/shard_map/ppermute | solution.py:455
  216.0 31.9 %collective-permute-start.20 = (bf16[256,768]{1,0:T(8,128)(2,1)}, bf16[256,768]{1,0:T(8,128)(2,1)}, u32[]{:S(2)}, u32[]{:S(2)}) collective-permute-start(bf16[256,768]{1,0:T(8,128)(2,1)} %get-tuple-element.166), channel_id=1, source_target_pairs={{0,1},{1,0},{2,3},{3,2},{4,5},{5,4},{6,7},{7,6},{8,9},{9,8},{10,11... | collective-permute-start | bytes 1179656 | tf_op jit(solution)/shard_map/ppermute | solution.py:455
  234.8 20.6 %collective-permute-start.38 = (bf16[192,1536]{1,0:T(8,128)(2,1)}, bf16[192,1536]{1,0:T(8,128)(2,1)}, u32[]{:S(2)}, u32[]{:S(2)}) collective-permute-start(bf16[192,1536]{1,0:T(8,128)(2,1)} %dynamic-slice_bitcast_fusion.6), channel_id=1, source_target_pairs={{0,4},{4,0},{8,12},{12,8},{16,20},{20,16},{24,28},{28,24},{1,5},{5... | collective-permute-start | bytes 1769480 | tf_op jit(solution)/shard_map/ppermute | solution.py:455
  236.2 27.1 %collective-permute-start.37 = (bf16[192,1536]{1,0:T(8,128)(2,1)}, bf16[192,1536]{1,0:T(8,128)(2,1)}, u32[]{:S(2)}, u32[]{:S(2)}) collective-permute-start(bf16[192,1536]{1,0:T(8,128)(2,1)} %dynamic-slice_bitcast_fusion.7), channel_id=1, source_target_pairs={{0,4},{4,0},{8,12},{12,8},{16,20},{20,16},{24,28},{28,24},{1,5},{5... | collective-permute-start | bytes 1769480 | tf_op jit(solution)/shard_map/ppermute | solution.py:455
  246.3 23.3 %collective-permute-start.75 = (bf16[384,768]{1,0:T(8,128)(2,1)}, bf16[384,768]{1,0:T(8,128)(2,1)}, u32[]{:S(2)}, u32[]{:S(2)}) collective-permute-start(bf16[384,768]{1,0:T(8,128)(2,1)} %dynamic-slice_bitcast_fusion.2), channel_id=1, source_target_pairs={{0,8},{4,12},{8,0},{12,4},{16,24},{20,28},{24,16},{28,20},{1,9},{5... | collective-permute-start | bytes 1769480 | tf_op jit(solution)/shard_map/ppermute | solution.py:455
  250.5 41.5 %collective-permute-start.31 = (bf16[256,768]{1,0:T(8,128)(2,1)}, bf16[256,768]{1,0:T(8,128)(2,1)}, u32[]{:S(2)}, u32[]{:S(2)}) collective-permute-start(bf16[256,768]{1,0:T(8,128)(2,1)} %get-tuple-element.199), channel_id=1, source_target_pairs={{0,1},{1,0},{2,3},{3,2},{4,5},{5,4},{6,7},{7,6},{8,9},{9,8},{10,11... | collective-permute-start | bytes 1179656 | tf_op jit(solution)/shard_map/ppermute | solution.py:455
  273.8 59.2 %collective-permute-start.76 = (bf16[192,768]{1,0:T(8,128)(2,1)}, bf16[192,768]{1,0:T(8,128)(2,1)}, u32[]{:S(2)}, u32[]{:S(2)}) collective-permute-start(bf16[192,768]{1,0:T(8,128)(2,1)} %dynamic-slice_bitcast_fusion.8), channel_id=1, source_target_pairs={{0,16},{4,20},{8,24},{12,28},{16,0},{20,4},{24,8},{28,12},{1,17},{... | collective-permute-start | bytes 884744 | tf_op jit(solution)/shard_map/ppermute | solution.py:455
  287.2 50.1 %collective-permute-start.42 = (bf16[48,1536]{1,0:T(8,128)(2,1)}, bf16[48,1536]{1,0:T(8,128)(2,1)}, u32[]{:S(2)}, u32[]{:S(2)}) collective-permute-start(bf16[48,1536]{1,0:T(8,128)(2,1)} %dynamic-slice_bitcast_fusion.16), channel_id=1, source_target_pairs={{0,16},{4,20},{8,24},{12,28},{16,0},{20,4},{24,8},{28,12},{1,17},{... | collective-permute-start | bytes 442376 | tf_op jit(solution)/shard_map/ppermute | solution.py:455
  289.0 48.3 %collective-permute-start.41 = (bf16[48,1536]{1,0:T(8,128)(2,1)}, bf16[48,1536]{1,0:T(8,128)(2,1)}, u32[]{:S(2)}, u32[]{:S(2)}) collective-permute-start(bf16[48,1536]{1,0:T(8,128)(2,1)} %dynamic-slice_bitcast_fusion.17), channel_id=1, source_target_pairs={{0,16},{4,20},{8,24},{12,28},{16,0},{20,4},{24,8},{28,12},{1,17},{... | collective-permute-start | bytes 442376 | tf_op jit(solution)/shard_map/ppermute | solution.py:455
  295.3 42.0 %collective-permute-start.36 = (bf16[768,768]{1,0:T(8,128)(2,1)}, bf16[768,768]{1,0:T(8,128)(2,1)}, u32[]{:S(2)}, u32[]{:S(2)}) collective-permute-start(bf16[768,768]{1,0:T(8,128)(2,1)} %dynamic-slice_bitcast_fusion), channel_id=1, source_target_pairs={{0,4},{4,0},{8,12},{12,8},{16,20},{20,16},{24,28},{28,24},{1,5},{5... | collective-permute-start | bytes 3538952 | tf_op jit(solution)/shard_map/ppermute | solution.py:455
  343.6 28.3 %collective-permute-start.43 = (bf16[256,768]{1,0:T(8,128)(2,1)S(1)}, bf16[256,768]{1,0:T(8,128)(2,1)S(1)}, u32[]{:S(2)}, u32[]{:S(2)}) collective-permute-start(bf16[256,768]{1,0:T(8,128)(2,1)S(1)} %copy-done.66), channel_id=1, source_target_pairs={{0,1},{1,0},{2,3},{3,2},{4,5},{5,4},{6,7},{7,6},{8,9},{9,8},{10,11... | collective-permute-start | bytes 1179656 | tf_op jit(solution)/shard_map/ppermute | solution.py:455
  348.5 23.4 %collective-permute-start.45 = (bf16[256,768]{1,0:T(8,128)(2,1)S(1)}, bf16[256,768]{1,0:T(8,128)(2,1)S(1)}, u32[]{:S(2)}, u32[]{:S(2)}) collective-permute-start(bf16[256,768]{1,0:T(8,128)(2,1)S(1)} %add_convert_fusion.5), channel_id=1, source_target_pairs={{0,2},{1,3},{2,0},{3,1},{4,6},{5,7},{6,4},{7,5},{8,10},{9,11},{10,... | collective-permute-start | bytes 1179656 | tf_op jit(solution)/shard_map/ppermute | solution.py:455
  366.1 37.0 %collective-permute-start.73 = (bf16[384,768]{1,0:T(8,128)(2,1)}, bf16[384,768]{1,0:T(8,128)(2,1)}, u32[]{:S(2)}, u32[]{:S(2)}) collective-permute-start(bf16[384,768]{1,0:T(8,128)(2,1)} %dynamic-slice_bitcast_fusion.3), channel_id=1, source_target_pairs={{0,8},{4,12},{8,0},{12,4},{16,24},{20,28},{24,16},{28,20},{1,9},{5... | collective-permute-start | bytes 1769480 | tf_op jit(solution)/shard_map/ppermute | solution.py:455
  398.0 19.0 %collective-permute-start.61 = (bf16[24,1536]{1,0:T(8,128)(2,1)S(1)}, bf16[24,1536]{1,0:T(8,128)(2,1)S(1)}, u32[]{:S(2)}, u32[]{:S(2)}) collective-permute-start(bf16[24,1536]{1,0:T(8,128)(2,1)S(1)} %fusion.44), channel_id=1, source_target_pairs={{0,16},{4,20},{8,24},{12,28},{16,0},{20,4},{24,8},{28,12},{1,17},{... | collective-permute-start | bytes 221192 | tf_op jit(solution)/shard_map/ppermute | solution.py:455
  398.0 22.8 %collective-permute-start.53 = (bf16[24,1536]{1,0:T(8,128)(2,1)S(1)}, bf16[24,1536]{1,0:T(8,128)(2,1)S(1)}, u32[]{:S(2)}, u32[]{:S(2)}) collective-permute-start(bf16[24,1536]{1,0:T(8,128)(2,1)S(1)} %fusion.45), channel_id=1, source_target_pairs={{0,16},{4,20},{8,24},{12,28},{16,0},{20,4},{24,8},{28,12},{1,17},{... | collective-permute-start | bytes 221192 | tf_op jit(solution)/shard_map/ppermute | solution.py:455
  405.0 61.8 %collective-permute-start.74 = (bf16[192,768]{1,0:T(8,128)(2,1)}, bf16[192,768]{1,0:T(8,128)(2,1)}, u32[]{:S(2)}, u32[]{:S(2)}) collective-permute-start(bf16[192,768]{1,0:T(8,128)(2,1)} %dynamic-slice_bitcast_fusion.9), channel_id=1, source_target_pairs={{0,16},{4,20},{8,24},{12,28},{16,0},{20,4},{24,8},{28,12},{1,17},{... | collective-permute-start | bytes 884744 | tf_op jit(solution)/shard_map/ppermute | solution.py:455
  420.9 17.8 %collective-permute-start.54 = (bf16[48,1536]{1,0:T(8,128)(2,1)S(1)}, bf16[48,1536]{1,0:T(8,128)(2,1)S(1)}, u32[]{:S(2)}, u32[]{:S(2)}) collective-permute-start(bf16[48,1536]{1,0:T(8,128)(2,1)S(1)} %pad_maximum_fusion.8), channel_id=1, source_target_pairs={{0,8},{4,12},{8,0},{12,4},{16,24},{20,28},{24,16},{28,20},{1,9},{5... | collective-permute-start | bytes 442376 | tf_op jit(solution)/shard_map/ppermute | solution.py:455
  443.6 17.9 %collective-permute-start.64 = (bf16[192,1536]{1,0:T(8,128)(2,1)S(1)}, bf16[192,1536]{1,0:T(8,128)(2,1)S(1)}, u32[]{:S(2)}, u32[]{:S(2)}) collective-permute-start(bf16[192,1536]{1,0:T(8,128)(2,1)S(1)} %pad_maximum_fusion.3), channel_id=1, source_target_pairs={{0,4},{4,0},{8,12},{12,8},{16,20},{20,16},{24,28},{28,24},{1,5},{5... | collective-permute-start | bytes 1769480 | tf_op jit(solution)/shard_map/ppermute | solution.py:455
  461.8 20.5 %collective-permute-start.65 = (bf16[384,1536]{1,0:T(8,128)(2,1)S(1)}, bf16[384,1536]{1,0:T(8,128)(2,1)}, u32[]{:S(2)}, u32[]{:S(2)}) collective-permute-start(bf16[384,1536]{1,0:T(8,128)(2,1)S(1)} %pad_maximum_fusion.1.refs_3_), channel_id=1, source_target_pairs={{0,1},{1,0},{2,3},{3,2},{4,5},{5,4},{6,7},{7,6},{8,9},{9,8},{10,11... | collective-permute-start | bytes 3538952 | tf_op jit(solution)/shard_map/ppermute | solution.py:455
  464.1 18.2 %collective-permute-start.57 = (bf16[384,1536]{1,0:T(8,128)(2,1)S(1)}, bf16[384,1536]{1,0:T(8,128)(2,1)}, u32[]{:S(2)}, u32[]{:S(2)}) collective-permute-start(bf16[384,1536]{1,0:T(8,128)(2,1)S(1)} %pad_maximum_fusion.refs_1_), channel_id=1, source_target_pairs={{0,1},{1,0},{2,3},{3,2},{4,5},{5,4},{6,7},{7,6},{8,9},{9,8},{10,11... | collective-permute-start | bytes 3538952 | tf_op jit(solution)/shard_map/ppermute | solution.py:455
  (129 other events, 924.0 us)
Sparse Core Ops, SparseCore 0:
  373.2 79.3 all-gather.2

commit v2 on v1

--- a/solution.py
+++ b/solution.py
@@ -11,6 +11,7 @@
 EPSILON = 1e-06
 NEGATIVE = -1e30
 LOG2E = 1.4426950408889634
+PIECES = 8
 GP = 2
 VMEM = 60 * 1024 * 1024
 F32 = jnp.float32
@@ -130,12 +131,13 @@
     )(*args)
 
 
-def attn_bwd_body(heads, blocks, layer, *refs):
-    (ga_ref, wout_ref, q_ref, k_ref, v_ref, p_ref, u_ref, tab_ref, tabt_ref, half_ref) = refs[:10]
+def attn_bwd_body(heads, blocks, layer, parts, *refs):
+    (ga_ref, wout_ref, q_ref, k_ref, v_ref, p_ref, u_ref, tab_ref, tabt_ref, place_ref) = refs[:10]
     wqkv_hbm, n1t_hbm, ot_hbm = refs[10:13]
     gn1_refs = refs[13 : 13 + blocks]
-    (ak_ref, as_ref, bk_ref, bs_ref, zpre_ref, zpost_ref) = refs[13 + blocks : 19 + blocks]
-    go_ref, got_ref, qt_ref, gq_acc, gk_acc, gv_acc, wqkv_ref, n1t_ref, ot_ref, sems = refs[19 + blocks :]
+    grad_refs = refs[13 + blocks : 13 + blocks + 2 * parts]
+    zpre_ref, zpost_ref = refs[13 + blocks + 2 * parts : 15 + blocks + 2 * parts]
+    go_ref, got_ref, qt_ref, gq_acc, gk_acc, gv_acc, wqkv_ref, n1t_ref, ot_ref, sems = refs[15 + blocks + 2 * parts :]
     step = pl.program_id(0)
     rows, width = q_ref.shape
     half = width // 2
@@ -199,20 +201,34 @@
             if r == 0:
                 gn1 = gn1 + dot_nt(gq, wqkv_ref[:, :width])
             gn1_refs[r][...] = gn1.astype(BF16)
-        which = half_ref[0]
-        for part, a_ref, b_ref in ((which, ak_ref, bk_ref), (1 - which, as_ref, bs_ref)):
-            mine = pl.ds(pl.multiple_of(part * half, half), half)
-            a_ref[:, :width] = dot_nt(n1t_ref[mine, :], gvt).astype(BF16)
-            a_ref[:, width:] = dot_nn(ot_ref[mine, :], ga).astype(BF16)
-            b_ref[:, :width] = dot_nn(n1t_ref[mine, :rows], gq).astype(BF16)
-            b_ref[:, width:] = dot_nt(n1t_ref[mine, :], gkt).astype(BF16)
-
-
-def attn_bwd(layer, blocks, ga, w_out, q, k, v, p, u, tab, tabt, half, w_qkv, n1t, ot):
+        per = half // PIECES
+        for side in range(2):
+            core = place_ref[0] if side == 0 else 1 - place_ref[0]
+            mine = pl.ds(pl.multiple_of(core * half, half), half)
+            n1t = n1t_ref[mine, :]
+            grads = (
+                lambda: dot_nn(n1t_ref[mine, :rows], gq),
+                lambda: dot_nt(n1t, gkt),
+                lambda: dot_nt(n1t, gvt),
+                lambda: dot_nn(ot_ref[mine, :], ga),
+            )
+            for index, grad in enumerate(grads):
+                part = index * parts // len(grads)
+                column = (index - part * (len(grads) // parts)) * width
+                value = grad().astype(BF16)
+                for piece in range(PIECES):
+                    there = pl.multiple_of((piece ^ place_ref[1 + part]) * per, per)
+                    grad_refs[2 * part + side][pl.ds(there, per), column : column + width] = value[
+                        piece * per : (piece + 1) * per
+                    ]
+
+
+def attn_bwd(layer, blocks, ga, w_out, q, k, v, p, u, tab, tabt, place, w_qkv, n1t, ot):
     rows, width = q.shape
     keys = k.shape[0]
     heads = p.shape[0]
-    args = (ga, w_out, q, k, v, p, u, tab, tabt, half, w_qkv, n1t, ot)
+    parts = place.shape[0] - 1
+    args = (ga, w_out, q, k, v, p, u, tab, tabt, place, w_qkv, n1t, ot)
     in_specs = [whole(a.shape) for a in args]
     in_specs[1] = layer_of(w_out, layer)
     in_specs[5] = pl.BlockSpec((GP, rows, keys), lambda i: (i, 0, 0))
@@ -223,11 +239,11 @@
     in_specs[10:13] = [pl.BlockSpec(memory_space=pl.ANY)] * 3
     out = (
         [((rows, width), BF16)] * blocks
-        + [((width // 2, 2 * width), BF16)] * 4
+        + [((width // 2, 4 // parts * width), BF16)] * (2 * parts)
         + [((heads, width), F32)] * 2
     )
     res = pl.pallas_call(
-        functools.partial(attn_bwd_body, heads, blocks, layer),
+        functools.partial(attn_bwd_body, heads, blocks, layer, parts),
         grid=(heads // GP,),
         in_specs=in_specs,
         out_specs=[whole(s) for s, _ in out],
@@ -250,76 +266,56 @@
         ),
         name="attn_bwd",
     )(*args)
-    return res[:blocks], res[blocks : blocks + 4], res[blocks + 4], res[blocks + 5]
-
-
-def expand_body(*refs):
-    which_ref, am_ref, ao_ref, bm_ref, bo_ref = refs[:5]
+    return res[:blocks], res[blocks:-2], res[-2], res[-1]
+
+
+def expand_body(parts, place_ref, *refs):
+    mine_refs, other_refs = refs[: 2 * parts : 2], refs[1 : 2 * parts : 2]
     qkv_ref, out_ref = refs[-2:]
-    step = pl.program_id(0)
-    width = out_ref.shape[2]
-    other = (step // (pl.num_programs(0) // 2)) != which_ref[0]
-
-    def write(a_ref, b_ref):
-        qkv_ref[0, :, : 2 * width] = b_ref[...].astype(F32)
-        qkv_ref[0, :, 2 * width :] = a_ref[:, :width].astype(F32)
-        out_ref[0] = a_ref[:, width:].astype(F32)
+    other = pl.program_id(0) // PIECES != place_ref[0]
+    width3 = qkv_ref.shape[2]
+
+    def write(part_refs):
+        column = 0
+        for ref in part_refs:
+            end = column + ref.shape[1]
+            cut = min(end, width3)
+            qkv_ref[0, :, column:cut] = ref[:, : cut - column].astype(F32)
+            if end > width3:
+                out_ref[0] = ref[:, cut - column :].astype(F32)
+            column = end
 
     @pl.when(other)
     def _():
-        write(ao_ref, bo_ref)
+        write(other_refs)
 
     @pl.when(jnp.logical_not(other))
     def _():
-        write(am_ref, bm_ref)
-
-
-def expand_first_body(both_ref, qkv_ref, out_ref):
-    width = out_ref.shape[2]
-    qkv_ref[0, :, : 2 * width] = both_ref[:, 2 * width :].astype(F32)
-    qkv_ref[0, :, 2 * width :] = both_ref[:, :width].astype(F32)
-    out_ref[0] = both_ref[:, width : 2 * width].astype(F32)
-
-
-def expand_first(layer, both):
-    rows, width4 = both.shape
-    width = width4 // 4
-    steps = 8
-    per = rows // steps
+        write(mine_refs)
+
+
+def expand(layer, place, mines, others, before=()):
+    half = mines[0].shape[0]
+    width = sum(m.shape[1] for m in mines) // 4
+    per = half // PIECES
+    in_specs, args = [], []
+    for part, pair in enumerate(zip(mines, others)):
+        for side, array in enumerate(pair):
+
+            def piece(i, place, part=part, side=side):
+                here = place[0] ^ side
+                wanted = jnp.where(i // PIECES == here, i % PIECES, (PIECES - 1) * (1 - here))
+                return wanted ^ place[1 + part], 0
+
+            in_specs.append(pl.BlockSpec((per, array.shape[1]), piece))
+            args.append(array)
+    first = 1 + len(args)
+    in_specs += [pl.BlockSpec(memory_space=pl.ANY)] * len(before)
     return pl.pallas_call(
-        expand_first_body,
-        grid=(steps,),
-        in_specs=[pl.BlockSpec((per, width4), lambda i: (i, 0))],
-        out_specs=[
-            pl.BlockSpec((1, per, 3 * width), lambda i: (layer, i, 0)),
-            pl.BlockSpec((1, per, width), lambda i: (layer, i, 0)),
-        ],
-        out_shape=[
-            jax.ShapeDtypeStruct((LAYERS, rows, 3 * width), F32),
-            jax.ShapeDtypeStruct((LAYERS, rows, width), F32),
-        ],
-        compiler_params=pltpu.CompilerParams(vmem_limit_bytes=VMEM),
-        cost_estimate=pl.CostEstimate(flops=0, bytes_accessed=14_000_000, transcendentals=0),
-        name="expand_first",
-    )(both)
-
-
-def expand(layer, a_mine, a_other, b_mine, b_other, which, before):
-    half, width2 = a_mine.shape
-    width = width2 // 2
-    steps = 8
-    each = steps // 2
-    per = half // each
-    mine = pl.BlockSpec((per, width2), lambda i, w: (jnp.clip(i - each * w[0], 0, each - 1), 0))
-    other = pl.BlockSpec((per, width2), lambda i, w: (jnp.clip(i - each * (1 - w[0]), 0, each - 1), 0))
-    in_specs = [mine, other, mine, other]
-    args = [which, a_mine, a_other, b_mine, b_other, *before]
-    in_specs += [pl.BlockSpec(memory_space=pl.ANY)] * 2
-    return pl.pallas_call(
-        expand_body,
+        functools.partial(expand_body, len(mines)),
         grid_spec=pltpu.PrefetchScalarGridSpec(
             num_scalar_prefetch=1,
-            grid=(steps,),
+            grid=(2 * PIECES,),
             in_specs=in_specs,
             out_specs=[
                 pl.BlockSpec((1, per, 3 * width), lambda i, w: (layer, i, 0)),
@@ -330,11 +326,11 @@
             jax.ShapeDtypeStruct((LAYERS, 2 * half, 3 * width), F32),
             jax.ShapeDtypeStruct((LAYERS, 2 * half, width), F32),
         ],
-        input_output_aliases={5: 0, 6: 1},
+        input_output_aliases={first + i: i for i in range(len(before))},
         compiler_params=pltpu.CompilerParams(vmem_limit_bytes=VMEM),
         cost_estimate=pl.CostEstimate(flops=0, bytes_accessed=14_000_000, transcendentals=0),
         name="expand",
-    )(*args)
+    )(place, *args, *before)
 
 
 def ffn_fwd_body(blocks, *refs):
@@ -530,62 +526,46 @@
         return [a.astype(F32) + b.astype(F32) for a, b in zip(self.kept, after(self.got, *done))]
 
 
-def halve(part, axis, bit):
-    return halve_end(*halve_begin(part, axis, bit))
-
-
-def double(part, axis, bit):
-    first = ((lax.axis_index(axis) // bit) & 1) == 0
-    got = swap(part, axis, bit)
-    return jnp.concatenate([jnp.where(first, part, got), jnp.where(first, got, part)], 0)
-
-
 def steps_of(axis):
     return [(axis, 1 << i) for i in range(lax.axis_size(axis).bit_length() - 1)]
 
 
-def sum_orders():
-    first, *tp_rest = steps_of("tp")
-    dp_first, *dp_rest = steps_of("dp")
-    return first, (tp_rest + [dp_first] + dp_rest, [dp_first] + tp_rest + dp_rest)
-
-
-def sum_begin(keep_a, send_a, keep_b, send_b):
-    first, _ = sum_orders()
-    return [halve_end(keep, swap(send, *first)) for keep, send in ((keep_a, send_a), (keep_b, send_b))]
-
-
-def sum_middle(parts, first_stage, last_stage=None):
-    _, orders = sum_orders()
-    for stage in range(len(orders[0]))[first_stage:last_stage]:
-        parts = [halve(part, *order[stage]) for part, order in zip(parts, orders)]
-    return parts
-
-
-def sum_end(parts):
-    first, orders = sum_orders()
-    for stage in range(len(orders[0]) - 1, -1, -1):
-        parts = [double(part, *order[stage]) for part, order in zip(parts, orders)]
-    others = [swap(part, *first) for part in parts]
-    return parts[0], others[0], parts[1], others[1]
-
-
-def gather_all(pieces, order):
-    both = lax.all_gather(jnp.concatenate(pieces, 1), ("dp", "tp"))
-    bits = len(order)
-    names = steps_of("dp")[::-1] + steps_of("tp")[::-1]
-    both = both.reshape((2,) * bits + both.shape[1:])
-    both = both.transpose([names.index(step) for step in order] + [bits, bits + 1])
-    return both.reshape(-1, both.shape[-1])
-
-
-def butterfly(value):
-    for axis in ("tp", "dp"):
-        bit = 1
-        while bit < lax.axis_size(axis):
-            value = value + swap(value, axis, bit)
-            bit *= 2
-    return value
+HALVINGS = PIECES.bit_length() - 1
+
+
+def place_of(order):
+    number = 0
+    for axis, bit in order[:HALVINGS]:
+        number = 2 * number + ((lax.axis_index(axis) // bit) & 1)
+    return number
+
+
+def sum_start(part, order, stage):
+    if stage < HALVINGS:
+        rows = part.shape[0] // 2
+        return part[:rows], swap(part[rows:], *order[stage])
+    return part, swap(part, *order[stage])
+
+
+def spread(part, got):
+    return jnp.concatenate([part, got], 0)
+
+
+class Butterfly:
+    def __init__(self, value):
+        self.value = value
+        self.steps = steps_of("tp") + steps_of("dp")
+        self.got = None
+
+    def start(self):
+        if self.steps:
+            self.got = swap(self.value, *self.steps.pop(0))
+            return [self.got]
+        return []
+
+    def end(self, got):
+        for g in got:
+            self.value = self.value + g
 
 
 def on_device(
@@ -615,7 +595,8 @@
         last = layer == LAYERS - 1
         n1_blocks = gather_blocks(rms(stream, gain_attn[layer]).astype(BF16))
         if last:
-            grad_near, grad_far = gather_near(after(cotangent[:, 0], n1_blocks[half]))
+            low, n1_blocks[half] = after((cotangent[:, 0], n1_blocks[half]))
+            grad_near, grad_far = gather_near(low)
         p, u, q, k, v, ot, n1t, middle, n2 = attn_fwd(
             layer,
             n1_blocks,
@@ -632,9 +613,10 @@
         out_a, hid_a, dgelu_a = ffn_fwd(layer, near, w_in, w_down)
         if last:
             gn2_a, gpre_a = ffn_bwd(layer, grad_near, dgelu_a, w_in, w_down)
-            far = after(far, gpre_a)
+            far, gpre_a = after((far, gpre_a))
             gf_blocks = grad_near + gather_far(grad_far)
-        n2_blocks = near + gather_far(after(far, hid_a))
+        far, hid_a = after((far, hid_a))
+        n2_blocks = near + gather_far(far)
         out_b, hid_b, dgelu_b = ffn_fwd(layer, n2_blocks[half:], w_in, w_down)
         kept.append((stream, n1t, p, u, q, k, v, ot, middle, n2_blocks, hid_a, hid_b, dgelu_a, dgelu_b))
         if not last:
@@ -651,18 +633,22 @@
         if not last:
             near, far = gather_near(grad_flow.astype(BF16))
             gn2_a, gpre_a = ffn_bwd(layer, near, dgelu_a, w_in, w_down)
-            gf_blocks = near + gather_far(after(far, gpre_a))
+            far, gpre_a, moving.got = after((far, gpre_a, moving.got))
+            (summed,) = moving.finish()
+            sharded[layer + 1] = (summed[:per], summed[per:].T)
+            gf_blocks = near + gather_far(far)
         gn2_b, gpre_b = ffn_bwd(layer, gf_blocks[half:], dgelu_b, w_in, w_down)
         if not last:
-            moving.advance(gpre_b)
-            summing.advance(gpre_b)
+            total_got, gpre_b = after((total_got, gpre_b))
+            total = halve_end(total_kept, total_got)
+            total_kept, total_got = sum_start(total, total_order, 1)
         own, far = scatter_begin([*gn2_a, *gn2_b])
         packed = ffn_grads(n2_blocks, gf_blocks, (hid_a, hid_b), (gpre_a, gpre_b), dp_size)
         far, packed = after((far, packed))
         if not last:
-            (summed,) = moving.finish(packed)
-            sharded[layer + 1] = (summed[:per], summed[per:].T)
-            summing.advance(packed)
+            total_got, packed = after((total_got, packed))
+            total = halve_end(total_kept, total_got)
+            total_kept, total_got = sum_start(total, total_order, 2)
         moving = Scatter([packed], steps_of("dp"))
         if last:
             own_y, far_y = scatter_begin(after([*out_a, *out_b], packed))
@@ -670,36 +656,31 @@
         grad_norm, grad_gffn = rms_back(gn2, middle, gain_ffn[layer])
         grad_middle = grad_flow + grad_norm
         ga = grad_middle.astype(BF16)
-        core = (tp_index & 1)[None]
+        if last:
+            orders = [steps_of("dp") + steps_of("tp")[1:]]
+        else:
+            (y_step, *dp_rest), x_steps = steps_of("dp"), steps_of("tp")[1:]
+            orders = [x_steps + [y_step] + dp_rest, [y_step] + x_steps + dp_rest]
+        place = jnp.stack([tp_index & 1] + [place_of(order) for order in orders])
         parts, grads, zpre, zpost = attn_bwd(
-            layer, tp_size, ga, w_out, q, k, v, p, u, tab, tabt, core, w_qkv, n1t, ot
+            layer, tp_size, ga, w_out, q, k, v, p, u, tab, tabt, place, w_qkv, n1t, ot
         )
+        core_step = steps_of("tp")[0]
         if last:
-            parts, grads, moving.got, far_y = after((parts, grads, moving.got, far_y))
+            parts, grads, moving.got, far_y, own_y = after((parts, grads, moving.got, far_y, own_y))
             y_out = (middle + (own_y + far_y.astype(F32))).astype(BF16)
+            keep, send = grads
+            total = halve_end(keep, swap(send, *core_step))
+            own, far = scatter_begin(parts)
+            moving.advance()
+            far, moving.got = after((far, moving.got), total)
+            moving.advance()
+            (total_order,), total_place = orders, place
+            total_kept, total_got = sum_start(total, total_order, 0)
         else:
-            parts, grads, moving.got, summing.got = after((parts, grads, moving.got, summing.got))
-        pieces = sum_begin(*grads)
-        own, far = scatter_begin(parts)
-        if last:
-            moving.advance()
-            far = after(far, *pieces)
-            order = steps_of("dp") + steps_of("tp")[1:]
-            summing = Scatter(pieces, order)
-        else:
-            reduced = summing.finish()
-            pieces = sum_middle(pieces, 0, 1)
-            far = after(far, *pieces)
-            moving.advance(*pieces)
-            reduced = after([r.astype(BF16) for r in reduced], *pieces)
-            gathered = gather_all(reduced, steps_of("tp")[:1] + order)
-            pieces = sum_middle(pieces, 1)
-            late = pieces
-            moving.advance(*pieces)
-            pieces = sum_end(pieces)
-            replicated = expand(0, *pieces, core, expand_first(1, gathered))
-            (summed,) = moving.finish()
-            sharded[layer] = (summed[:per], summed[per:].T)
+            parts, grads, moving.got, total_got = after((parts, grads, moving.got, total_got))
+        if not last:
+            break
         gn1 = (own + far.astype(F32)).astype(BF16).astype(F32)
         grad_norm, grad_gattn = rms_back(gn1, stream, gain_attn[layer])
         grad_flow = grad_middle + grad_norm
@@ -707,6 +688,29 @@
         grad_mpost = jnp.sum(zpost.reshape(heads, heads, head_size), -1)
         small[layer] = (grad_mpre, grad_mpost, grad_gattn, grad_gffn)
 
+    total = halve_end(total_kept, total_got)
+    got = [swap(send, *core_step) for send in grads[1::2]]
+    for stage in range(HALVINGS, len(total_order)):
+        total_got = swap(total, *total_order[stage])
+        got, total_got = after((got, total_got))
+        total = halve_end(total, total_got)
+    pieces = [halve_end(keep, g) for keep, g in zip(grads[::2], got)]
+    own, far = scatter_begin(parts)
+    for stage in range(HALVINGS):
+        kept, got = zip(*[sum_start(part, order, stage) for part, order in zip(pieces, orders)])
+        total_got = swap(total, *total_order[HALVINGS - 1 - stage])
+        if stage < HALVINGS - 1:
+            got, total_got = after((got, total_got))
+            total = spread(total, total_got)
+        pieces = [halve_end(a, b) for a, b in zip(kept, after(got))]
+        if stage == 0:
+            far, pieces = after((far, pieces))
+            gn1 = (own + far.astype(F32)).astype(BF16).astype(F32)
+            grad_norm, grad_gattn = rms_back(gn1, stream, gain_attn[layer])
+            grad_flow = grad_middle + grad_norm
+            grad_mpre = jnp.sum(zpre.reshape(heads, heads, head_size), -1).T * (head_size**-0.5)
+            grad_mpost = jnp.sum(zpost.reshape(heads, heads, head_size), -1)
+            small[layer] = (grad_mpre, grad_mpost, grad_gattn, grad_gffn)
     mixes = jnp.concatenate([a.reshape(-1) for s in small for a in s[:2]])
     count = mixes.shape[0]
     mix_rows = -(-count // width)
@@ -715,7 +719,41 @@
         + [g[None] for s in small for g in s[2:]]
     )
     flat = jnp.pad(flat, ((0, -flat.shape[0] % 8), (0, 0)))
-    flat = butterfly(after(flat, *late))
+    flat, pieces = after((flat, pieces))
+    flat = Butterfly(flat)
+    for stage in range(HALVINGS, len(orders[0])):
+        got = [swap(part, *order[stage]) for part, order in zip(pieces, orders)]
+        flat_got = flat.start()
+        if stage == HALVINGS:
+            got, flat_got, total_got = after((got, flat_got, total_got))
+            total = spread(total, total_got)
+        got, flat_got = after((got, flat_got))
+        flat.end(flat_got)
+        pieces = [halve_end(a, b) for a, b in zip(pieces, got)]
+    total_other = swap(total, *core_step)
+    moving.advance(*pieces)
+    for stage in range(HALVINGS - 1, -1, -1):
+        got = [swap(part, *order[stage]) for part, order in zip(pieces, orders)]
+        flat_got = flat.start()
+        if stage == HALVINGS - 1:
+            got, flat_got, total_other = after((got, flat_got, total_other))
+        if stage < HALVINGS - 1:
+            got, moving.got = after((got, moving.got))
+            moving.advance()
+        if stage == 0:
+            replicated = expand(1, total_place, [total], [total_other])
+            got, flat_got, replicated = after((got, flat_got, replicated))
+        got, flat_got = after((got, flat_got))
+        flat.end(flat_got)
+        pieces = [spread(a, b) for a, b in zip(pieces, got)]
+    got = [swap(part, *core_step) for part in pieces]
+    while flat.steps:
+        flat.end(flat.start())
+    flat = flat.value
+    (summed,) = moving.finish()
+    sharded[0] = (summed[:per], summed[per:].T)
+    got, sharded = after((got, sharded))
+    replicated = expand(0, place, pieces, got, replicated)
     mixes = flat[:mix_rows].reshape(-1)[:count].reshape(LAYERS, 2, heads, heads)
     gains = flat[mix_rows : mix_rows + 2 * LAYERS].reshape(LAYERS, 2, width)
     return (

time: 507 us -> 483 us (0.953)
  waiting for transfers between devices: 141 us -> 112 us
  between operations: 15.9 us -> 2.42 us
  other arithmetic: 43 us -> 54.5 us
  Pallas kernels: 193 us -> 202 us
    ppermute x77 -> x74, waiting for transfers between devices: 141 us -> 112 us  [swap(): return lax.ppermute(value, axis, [(i, i ^ bit) for i in range(size)])]
    squeeze x22 -> x6, local copies, waits for them, and re-layouts: 12.8 us -> 2.02 us  [halve_begin(): sent = lax.dynamic_index_in_dim(pair, 1 - mine, 0, keepdims=False)]
    pallas_call x4, Pallas kernels: 87.4 us -> 96.8 us  [the longest x2 72.1 us: attn_bwd(): pl.pallas_call(functools.partial(attn_bwd_body, heads, blocks, layer, par...]
    unnamed x156 -> x214, local copies, waits for them, and re-layouts: 12.7 us -> 19.2 us
    slice x0 -> x9, local copies, waits for them, and re-layouts: none -> 5.93 us  [sum_start(): return (part[:rows], swap(part[rows:], *order[stage]))]
    concatenate x9 -> x10, other arithmetic: 0.98 us -> 6.76 us  [the longest x9 6.75 us: spread(): return jnp.concatenate([part, got], 0)]
    ppermute x77 -> x74, starting transfers between devices: 61.7 us -> 63.3 us  [swap(): return lax.ppermute(value, axis, [(i, i ^ bit) for i in range(size)])]
    convert_element_type x22 -> x19, other arithmetic: 20.4 us -> 20.5 us  [halve_end(): return (kept.astype(F32) + got.astype(F32)).astype(BF16)]
  transfers between devices with their start and end apart: 78 -> 74, of which waited for: 33 -> 30; matrix products, arithmetic and copies ran while one was open for 15% -> 14% of each run, Pallas kernels for 30% -> 32%
where the time goes in v2:
time: 483 us; the launch traced here: 473 us
  Pallas kernels  202 us (42%)
  waiting for transfers between devices  112 us (23%)
  starting transfers between devices  63.3 us (13%)
  other arithmetic  54.5 us (11%)
  local copies, waits for them, and re-layouts  38.8 us (8%)
    ppermute x74, waiting for transfers between devices, swap(): return lax.ppermute(value, axis, [(i, i ^ bit) for i in range(size)])  112 us
    pallas_call x2, Pallas kernels, attn_bwd(): pl.pallas_call(functools.partial(attn_bwd_body, heads, blocks, layer, par...  72.1 us
    ppermute x74, starting transfers between devices, swap(): return lax.ppermute(value, axis, [(i, i ^ bit) for i in range(size)])  63.3 us
    pallas_call x2, Pallas kernels, attn_fwd(): pl.pallas_call(functools.partial(attn_fwd_body, blocks, heads, layer), gr...  55.1 us
    pallas_call x2, Pallas kernels, expand(): pl.pallas_call(functools.partial(expand_body, len(mines)), grid_spec=pltp...  24.7 us
    convert_element_type x19, other arithmetic, halve_end(): return (kept.astype(F32) + got.astype(F32)).astype(BF16)  20.5 us
    unnamed x214, local copies, waits for them, and re-layouts  19.2 us
    pallas_call x4, Pallas kernels, ffn_bwd(): pl.pallas_call(functools.partial(ffn_bwd_body, blocks), grid=(1,), in_spe...  18.8 us
  transfers between devices with their start and end apart: 74, of which 30 were waited for; matrix products, arithmetic and copies ran while one was open for 14% of the time, Pallas kernels for 32%

profile of v2, /device:TPU:0, one launch (start us, length us, event | category | flops | bytes accessed | tf_op | source)
XLA Modules:
  0.0 473.3 jit_solution(17856604200837201425)
XLA Ops:
  7.1 8.9 %collective-permute-done.1.refs_2_ = bf16[256,768]{1,0:T(8,128)(2,1)S(1)} collective-permute-done((bf16[256,768]{1,0:T(8,128)(2,1)S(1)}, bf16[256,768]{1,0:T(8,128)(2,1)S(1)}, u32[]{:S(2)}, u32[]{:S(2)}) %collective-permute-start.1) | collective-permute-done | bytes 393248 | tf_op jit(solution)/shard_map/ppermute | solution.py:451
  20.9 27.4 %attn_fwd.2 = (bf16[12,256,1024]{2,1,0:T(8,128)(2,1)}, bf16[12,256,768]{2,1,0:T(8,128)(2,1)}, bf16[256,768]{1,0:T(8,128)(2,1)}, bf16[1024,768]{1,0:T(8,128)(2,1)...) custom-call(bf16[256,768]{1,0:T(8,128)(2,1)} %copy-done.53, ...), custom_call_target="tpu_custom_call" | custom-call | flops 9663676416 | bytes 20000000 | tf_op jit(solution)/shard_map/attn_fwd/pallas_call | solution.py:119
  51.3 4.6 ffn_fwd.4
  72.0 9.4 %collective-permute-done.8 = bf16[256,768]{1,0:T(8,128)(2,1)S(1)} collective-permute-done((bf16[256,768]{1,0:T(8,128)(2,1)S(1)}, bf16[256,768]{1,0:T(8,128)(2,1)S(1)}, u32[]{:S(2)}, u32[]{:S(2)}) %collective-permute-start.8) | collective-permute-done | bytes 393248 | tf_op jit(solution)/shard_map/ppermute | solution.py:451
  84.3 8.6 %collective-permute-done.10.refs_2_ = bf16[256,768]{1,0:T(8,128)(2,1)S(1)} collective-permute-done((bf16[256,768]{1,0:T(8,128)(2,1)S(1)}, bf16[256,768]{1,0:T(8,128)(2,1)S(1)}, u32[]{:S(2)}, u32[]{:S(2)}) %collective-permute-start.10) | collective-permute-done | bytes 393248 | tf_op jit(solution)/shard_map/ppermute | solution.py:451
  96.0 27.7 %attn_fwd.3 = (bf16[12,256,1024]{2,1,0:T(8,128)(2,1)}, bf16[12,256,768]{2,1,0:T(8,128)(2,1)}, bf16[256,768]{1,0:T(8,128)(2,1)}, bf16[1024,768]{1,0:T(8,128)(2,1)...) custom-call(bf16[256,768]{1,0:T(8,128)(2,1)} %copy-done.61, ...), custom_call_target="tpu_custom_call" | custom-call | flops 9663676416 | bytes 20000000 | tf_op jit(solution)/shard_map/attn_fwd/pallas_call | solution.py:119
  131.0 4.7 ffn_bwd.4
  138.1 4.6 ffn_fwd.7
  143.5 4.7 ffn_bwd.5
  151.4 6.9 %ffn_grads.2 = bf16[1536,768]{1,0:T(8,128)(2,1)} custom-call(bf16[256,768]{1,0:T(8,128)(2,1)} %get-tuple-element.199.refs_0_, bf16[256,768]{1,0:T(8,128)(2,1)} %copy-done.67, bf16[256,768]{1,0:T(8,128)(2,1)} %copy-done.68, bf16[256,768]{1,0:T(8,128)(2,1)} %copy-done.69, bf16[256,768]{1,0:T(8,128)(2,1)} %bitcast.104, bf16[256,768]{1,0:T(8,128)(2,1)} %copy-done.47, ...), custom_call_target="tpu_custom_call" | custom-call | flops 2415919104 | bytes 9000000 | tf_op jit(solution)/shard_map/ffn_grads/pallas_call | solution.py:435
  168.6 36.0 %attn_bwd.2 = (bf16[256,768]{1,0:T(8,128)(2,1)}, bf16[256,768]{1,0:T(8,128)(2,1)}, bf16[256,768]{1,0:T(8,128)(2,1)}, bf16[256,768]{1,0:T(8,128)(2,1)}, bf16[384,...) custom-call(bf16[256,768]{1,0:T(8,128)(2,1)} %get-tuple-element.407.refs_0_, ...), custom_call_target="tpu_custom_call" | custom-call | flops 38654705664 | bytes 20000000 | tf_op jit(solution)/shard_map/attn_bwd/pallas_call | solution.py:245
  214.8 8.7 %collective-permute-done.28 = bf16[384,768]{1,0:T(8,128)(2,1)S(1)} collective-permute-done((bf16[384,768]{1,0:T(8,128)(2,1)S(1)}, bf16[384,768]{1,0:T(8,128)(2,1)S(1)}, u32[]{:S(2)}, u32[]{:S(2)}) %collective-permute-start.28) | collective-permute-done | bytes 589856 | tf_op jit(solution)/shard_map/ppermute | solution.py:451
  233.5 4.7 ffn_bwd.6
  238.2 7.0 %collective-permute-done.33 = bf16[192,768]{1,0:T(8,128)(2,1)} collective-permute-done((bf16[192,768]{1,0:T(8,128)(2,1)}, bf16[192,768]{1,0:T(8,128)(2,1)}, u32[]{:S(2)}, u32[]{:S(2)}) %collective-permute-start.33) | collective-permute-done | bytes 294944 | tf_op jit(solution)/shard_map/ppermute | solution.py:451
  247.9 4.7 %ffn_bwd.7 = (bf16[256,768]{1,0:T(8,128)(2,1)}, bf16[256,768]{1,0:T(8,128)(2,1)}, bf16[512,768]{1,0:T(8,128)(2,1)}) custom-call(bf16[256,768]{1,0:T(8,128)(2,1)} %collective-permute-done.32.refs_0_.refs_6_, bf16[256,768]{1,0:T(8,128)(2,1)} %copy-done.51, bf16[512,768]{1,0:T(8,128)(2,1)} %get-tuple-element.254.refs_2_, bf16[2,768,768]{2,1,0:T(8,128)(2,1)} %refs_3_.15, ...), custom_call_target="tpu_custom_call" | custom-call | flops 1207959552 | bytes 6000000 | tf_op jit(solution)/shard_map/ffn_bwd/pallas_call | solution.py:400
  254.5 5.9 %collective-permute-done.37 = bf16[192,3072]{1,0:T(8,128)(2,1)} collective-permute-done((bf16[192,3072]{1,0:T(8,128)(2,1)}, bf16[192,3072]{1,0:T(8,128)(2,1)}, u32[]{:S(2)}, u32[]{:S(2)}) %collective-permute-start.37) | collective-permute-done | bytes 1179680 | tf_op jit(solution)/shard_map/ppermute | solution.py:451
  267.7 6.8 %ffn_grads.3 = bf16[1536,768]{1,0:T(8,128)(2,1)} custom-call(bf16[256,768]{1,0:T(8,128)(2,1)} %get-tuple-element.186.refs_0_, bf16[256,768]{1,0:T(8,128)(2,1)} %copy-done.64, bf16[256,768]{1,0:T(8,128)(2,1)} %copy-done.65, bf16[256,768]{1,0:T(8,128)(2,1)} %copy-done.66, bf16[256,768]{1,0:T(8,128)(2,1)} %copy-done.31, bf16[256,768]{1,0:T(8,128)(2,1)} %copy-done.49, ...), custom_call_target="tpu_custom_call" | custom-call | flops 2415919104 | bytes 9000000 | tf_op jit(solution)/shard_map/ffn_grads/pallas_call | solution.py:435
  283.4 36.1 %attn_bwd.3 = (bf16[256,768]{1,0:T(8,128)(2,1)}, bf16[256,768]{1,0:T(8,128)(2,1)}, bf16[256,768]{1,0:T(8,128)(2,1)}, bf16[256,768]{1,0:T(8,128)(2,1)}, bf16[384,...) custom-call(bf16[256,768]{1,0:T(8,128)(2,1)} %get-tuple-element.403., ...), custom_call_target="tpu_custom_call" | custom-call | flops 38654705664 | bytes 20000000 | tf_op jit(solution)/shard_map/attn_bwd/pallas_call | solution.py:245
  324.4 6.7 %collective-permute-done.46 = bf16[48,3072]{1,0:T(8,128)(2,1)S(1)} collective-permute-done((bf16[48,3072]{1,0:T(8,128)(2,1)S(1)}, bf16[48,3072]{1,0:T(8,128)(2,1)S(1)}, u32[]{:S(2)}, u32[]{:S(2)}) %collective-permute-start.46) | collective-permute-done | bytes 294944 | tf_op jit(solution)/shard_map/ppermute | solution.py:451
  347.7 6.9 %collective-permute-done.49 = bf16[48,3072]{1,0:T(8,128)(2,1)S(1)} collective-permute-done((bf16[48,3072]{1,0:T(8,128)(2,1)S(1)}, bf16[48,3072]{1,0:T(8,128)(2,1)S(1)}, u32[]{:S(2)}, u32[]{:S(2)}) %collective-permute-start.49) | collective-permute-done | bytes 294944 | tf_op jit(solution)/shard_map/ppermute | solution.py:451
  386.8 8.2 %collective-permute-done.55 = bf16[48,1536]{1,0:T(8,128)(2,1)S(1)} collective-permute-done((bf16[48,1536]{1,0:T(8,128)(2,1)S(1)}, bf16[48,1536]{1,0:T(8,128)(2,1)S(1)}, u32[]{:S(2)}, u32[]{:S(2)}) %collective-permute-start.55) | collective-permute-done | bytes 147488 | tf_op jit(solution)/shard_map/ppermute | solution.py:451
  418.0 5.2 %collective-permute-done.65 = bf16[384,768]{1,0:T(8,128)(2,1)S(1)} collective-permute-done((bf16[384,768]{1,0:T(8,128)(2,1)S(1)}, bf16[384,768]{1,0:T(8,128)(2,1)S(1)}, u32[]{:S(2)}, u32[]{:S(2)}) %collective-permute-start.65) | collective-permute-done | bytes 589856 | tf_op jit(solution)/shard_map/ppermute | solution.py:451
  431.4 12.1 %expand.2 = (f32[2,768,2304]{2,1,0:T(8,128)}, f32[2,768,768]{2,1,0:T(8,128)}) custom-call(s32[2]{0:T(128)} %pad_add_fusion.3.refs_9_.place_ref, bf16[384,3072]{1,0:T(8,128)(2,1)} %copy-done.5, bf16[384,3072]{1,0:T(8,128)(2,1)} %collective-permute-done.62.refs_1_), custom_call_target="tpu_custom_call" | custom-call | bytes 14000000 | tf_op jit(solution)/shard_map/expand/pallas_call | solution.py:314
  460.3 12.5 %expand.3 = (f32[2,768,2304]{2,1,0:T(8,128)}, f32[2,768,768]{2,1,0:T(8,128)}) custom-call(s32[3]{0:T(128)} %pad_add_fusion.4.refs_9_.place_ref, bf16[384,1536]{1,0:T(8,128)(2,1)} %copy-done.8, bf16[384,1536]{1,0:T(8,128)(2,1)} %collective-permute-done.71.refs_1_, bf16[384,1536]{1,0:T(8,128)(2,1)} %copy-done.7, ...), custom_call_target="tpu_custom_call", output_to_operand_aliasing={{0}: (5, {}), {1}: (6, {})} | custom-call | bytes 14000000 | tf_op jit(solution)/shard_map/expand/pallas_call | solution.py:314
  (489 shorter events, 201.8 us)
Async XLA Ops:
  93.0 30.7 %collective-permute-start.12 = (bf16[256,768]{1,0:T(8,128)(2,1)S(1)}, bf16[256,768]{1,0:T(8,128)(2,1)S(1)}, u32[]{:S(2)}, u32[]{:S(2)}) collective-permute-start(bf16[256,768]{1,0:T(8,128)(2,1)S(1)} %bitcast.105), channel_id=1, source_target_pairs={{0,1},{1,0},{2,3},{3,2},{4,5},{5,4},{6,7},{7,6},{8,9},{9,8},{10,11... | collective-permute-start | bytes 1179656 | tf_op jit(solution)/shard_map/ppermute | solution.py:451
  93.5 30.2 %collective-permute-start.13 = (bf16[256,768]{1,0:T(8,128)(2,1)S(1)}, bf16[256,768]{1,0:T(8,128)(2,1)S(1)}, u32[]{:S(2)}, u32[]{:S(2)}) collective-permute-start(bf16[256,768]{1,0:T(8,128)(2,1)S(1)} %bitcast.106), channel_id=1, source_target_pairs={{0,2},{1,3},{2,0},{3,1},{4,6},{5,7},{6,4},{7,5},{8,10},{9,11},{10,... | collective-permute-start | bytes 1179656 | tf_op jit(solution)/shard_map/ppermute | solution.py:451
  162.0 42.6 %collective-permute-start.24 = (bf16[256,768]{1,0:T(8,128)(2,1)}, bf16[256,768]{1,0:T(8,128)(2,1)S(1)}, u32[]{:S(2)}, u32[]{:S(2)}) collective-permute-start(bf16[256,768]{1,0:T(8,128)(2,1)} %get-tuple-element.237), channel_id=1, source_target_pairs={{0,1},{1,0},{2,3},{3,2},{4,5},{5,4},{6,7},{7,6},{8,9},{9,8},{10,11... | collective-permute-start | bytes 1179656 | tf_op jit(solution)/shard_map/ppermute | solution.py:451
  165.3 40.3 %collective-permute-start.21 = (bf16[768,768]{1,0:T(8,128)(2,1)}, bf16[768,768]{1,0:T(8,128)(2,1)}, u32[]{:S(2)}, u32[]{:S(2)}) collective-permute-start(bf16[768,768]{1,0:T(8,128)(2,1)} %dynamic-slice_bitcast_fusion.1), channel_id=1, source_target_pairs={{0,4},{4,0},{8,12},{12,8},{16,20},{20,16},{24,28},{28,24},{1,5},{5... | collective-permute-start | bytes 3538952 | tf_op jit(solution)/shard_map/ppermute | solution.py:451
  168.0 37.7 %collective-permute-start.23 = (bf16[256,768]{1,0:T(8,128)(2,1)S(1)}, bf16[256,768]{1,0:T(8,128)(2,1)}, u32[]{:S(2)}, u32[]{:S(2)}) collective-permute-start(bf16[256,768]{1,0:T(8,128)(2,1)S(1)} %add_convert_fusion.14), channel_id=1, source_target_pairs={{0,2},{1,3},{2,0},{3,1},{4,6},{5,7},{6,4},{7,5},{8,10},{9,11},{10,... | collective-permute-start | bytes 1179656 | tf_op jit(solution)/shard_map/ppermute | solution.py:451
  208.2 15.4 %collective-permute-start.28 = (bf16[384,768]{1,0:T(8,128)(2,1)S(1)}, bf16[384,768]{1,0:T(8,128)(2,1)S(1)}, u32[]{:S(2)}, u32[]{:S(2)}) collective-permute-start(bf16[384,768]{1,0:T(8,128)(2,1)S(1)} %dynamic-slice_bitcast_fusion.3), channel_id=1, source_target_pairs={{0,8},{4,12},{8,0},{12,4},{16,24},{20,28},{24,16},{28,20},{1,9},{5... | collective-permute-start | bytes 1769480 | tf_op jit(solution)/shard_map/ppermute | solution.py:451
  225.3 19.9 %collective-permute-start.32 = (bf16[256,768]{1,0:T(8,128)(2,1)S(1)}, bf16[256,768]{1,0:T(8,128)(2,1)}, u32[]{:S(2)}, u32[]{:S(2)}) collective-permute-start(bf16[256,768]{1,0:T(8,128)(2,1)S(1)} %fusion.32.refs_0_.refs_4_), channel_id=1, source_target_pairs={{0,2},{1,3},{2,0},{3,1},{4,6},{5,7},{6,4},{7,5},{8,10},{9,11},{10,... | collective-permute-start | bytes 1179656 | tf_op jit(solution)/shard_map/ppermute | solution.py:451
  228.5 16.7 %collective-permute-start.33 = (bf16[192,768]{1,0:T(8,128)(2,1)}, bf16[192,768]{1,0:T(8,128)(2,1)}, u32[]{:S(2)}, u32[]{:S(2)}) collective-permute-start(bf16[192,768]{1,0:T(8,128)(2,1)} %dynamic-slice_bitcast_fusion.5), channel_id=1, source_target_pairs={{0,16},{4,20},{8,24},{12,28},{16,0},{20,4},{24,8},{28,12},{1,17},{... | collective-permute-start | bytes 884744 | tf_op jit(solution)/shard_map/ppermute | solution.py:451
  232.2 28.1 %collective-permute-start.37 = (bf16[192,3072]{1,0:T(8,128)(2,1)}, bf16[192,3072]{1,0:T(8,128)(2,1)}, u32[]{:S(2)}, u32[]{:S(2)}) collective-permute-start(bf16[192,3072]{1,0:T(8,128)(2,1)} %slice.137), channel_id=1, source_target_pairs={{0,4},{4,0},{8,12},{12,8},{16,20},{20,16},{24,28},{28,24},{1,5},{5... | collective-permute-start | bytes 3538952 | tf_op jit(solution)/shard_map/ppermute | solution.py:451
  254.1 20.4 %collective-permute-start.31 = (bf16[256,768]{1,0:T(8,128)(2,1)}, bf16[256,768]{1,0:T(8,128)(2,1)}, u32[]{:S(2)}, u32[]{:S(2)}) collective-permute-start(bf16[256,768]{1,0:T(8,128)(2,1)} %get-tuple-element.250), channel_id=1, source_target_pairs={{0,1},{1,0},{2,3},{3,2},{4,5},{5,4},{6,7},{7,6},{8,9},{9,8},{10,11... | collective-permute-start | bytes 1179656 | tf_op jit(solution)/shard_map/ppermute | solution.py:451
  266.1 14.4 %collective-permute-start.38 = (bf16[96,3072]{1,0:T(8,128)(2,1)}, bf16[96,3072]{1,0:T(8,128)(2,1)}, u32[]{:S(2)}, u32[]{:S(2)}) collective-permute-start(bf16[96,3072]{1,0:T(8,128)(2,1)} %slice.139), channel_id=1, source_target_pairs={{0,8},{4,12},{8,0},{12,4},{16,24},{20,28},{24,16},{28,20},{1,9},{5... | collective-permute-start | bytes 1769480 | tf_op jit(solution)/shard_map/ppermute | solution.py:451
  282.4 37.1 %collective-permute-start.40 = (bf16[48,3072]{1,0:T(8,128)(2,1)}, bf16[48,3072]{1,0:T(8,128)(2,1)}, u32[]{:S(2)}, u32[]{:S(2)}) collective-permute-start(bf16[48,3072]{1,0:T(8,128)(2,1)} %slice.141), channel_id=1, source_target_pairs={{0,16},{4,20},{8,24},{12,28},{16,0},{20,4},{24,8},{28,12},{1,17},{... | collective-permute-start | bytes 884744 | tf_op jit(solution)/shard_map/ppermute | solution.py:451
  282.9 36.7 %collective-permute-start.39 = (bf16[768,768]{1,0:T(8,128)(2,1)S(1)}, bf16[768,768]{1,0:T(8,128)(2,1)S(1)}, u32[]{:S(2)}, u32[]{:S(2)}) collective-permute-start(bf16[768,768]{1,0:T(8,128)(2,1)S(1)} %dynamic-slice_bitcast_fusion), channel_id=1, source_target_pairs={{0,4},{4,0},{8,12},{12,8},{16,20},{20,16},{24,28},{28,24},{1,5},{5... | collective-permute-start | bytes 3538952 | tf_op jit(solution)/shard_map/ppermute | solution.py:451
  324.1 21.8 %collective-permute-start.42 = (bf16[256,768]{1,0:T(8,128)(2,1)}, bf16[256,768]{1,0:T(8,128)(2,1)}, u32[]{:S(2)}, u32[]{:S(2)}) collective-permute-start(bf16[256,768]{1,0:T(8,128)(2,1)} %get-tuple-element.285), channel_id=1, source_target_pairs={{0,1},{1,0},{2,3},{3,2},{4,5},{5,4},{6,7},{7,6},{8,9},{9,8},{10,11... | collective-permute-start | bytes 1179656 | tf_op jit(solution)/shard_map/ppermute | solution.py:451
  335.0 19.7 %collective-permute-start.48 = (bf16[192,1536]{1,0:T(8,128)(2,1)}, bf16[192,1536]{1,0:T(8,128)(2,1)}, u32[]{:S(2)}, u32[]{:S(2)}) collective-permute-start(bf16[192,1536]{1,0:T(8,128)(2,1)} %slice.145), channel_id=1, source_target_pairs={{0,4},{4,0},{8,12},{12,8},{16,20},{20,16},{24,28},{28,24},{1,5},{5... | collective-permute-start | bytes 1769480 | tf_op jit(solution)/shard_map/ppermute | solution.py:451
  337.7 16.9 %collective-permute-start.47 = (bf16[192,1536]{1,0:T(8,128)(2,1)}, bf16[192,1536]{1,0:T(8,128)(2,1)}, u32[]{:S(2)}, u32[]{:S(2)}) collective-permute-start(bf16[192,1536]{1,0:T(8,128)(2,1)} %slice.144), channel_id=1, source_target_pairs={{0,2},{1,3},{2,0},{3,1},{4,6},{5,7},{6,4},{7,5},{8,10},{9,11},{10,... | collective-permute-start | bytes 1769480 | tf_op jit(solution)/shard_map/ppermute | solution.py:451
  339.2 15.4 %collective-permute-start.49 = (bf16[48,3072]{1,0:T(8,128)(2,1)S(1)}, bf16[48,3072]{1,0:T(8,128)(2,1)S(1)}, u32[]{:S(2)}, u32[]{:S(2)}) collective-permute-start(bf16[48,3072]{1,0:T(8,128)(2,1)S(1)} %add_convert_fusion.20), channel_id=1, source_target_pairs={{0,16},{4,20},{8,24},{12,28},{16,0},{20,4},{24,8},{28,12},{1,17},{... | collective-permute-start | bytes 884744 | tf_op jit(solution)/shard_map/ppermute | solution.py:451
  347.1 13.9 %collective-permute-start.43 = (bf16[256,768]{1,0:T(8,128)(2,1)S(1)}, bf16[256,768]{1,0:T(8,128)(2,1)S(1)}, u32[]{:S(2)}, u32[]{:S(2)}) collective-permute-start(bf16[256,768]{1,0:T(8,128)(2,1)S(1)} %add_convert_fusion.8), channel_id=1, source_target_pairs={{0,2},{1,3},{2,0},{3,1},{4,6},{5,7},{6,4},{7,5},{8,10},{9,11},{10,... | collective-permute-start | bytes 1179656 | tf_op jit(solution)/shard_map/ppermute | solution.py:451
  355.5 15.7 %collective-permute-start.52 = (bf16[96,3072]{1,0:T(8,128)(2,1)}, bf16[96,3072]{1,0:T(8,128)(2,1)S(1)}, u32[]{:S(2)}, u32[]{:S(2)}) collective-permute-start(bf16[96,3072]{1,0:T(8,128)(2,1)} %pad_maximum_fusion.4), channel_id=1, source_target_pairs={{0,8},{4,12},{8,0},{12,4},{16,24},{20,28},{24,16},{28,20},{1,9},{5... | collective-permute-start | bytes 1769480 | tf_op jit(solution)/shard_map/ppermute | solution.py:451
  372.4 25.9 %collective-permute-start.58 = (bf16[192,3072]{1,0:T(8,128)(2,1)}, bf16[192,3072]{1,0:T(8,128)(2,1)}, u32[]{:S(2)}, u32[]{:S(2)}) collective-permute-start(bf16[192,3072]{1,0:T(8,128)(2,1)} %pad_maximum_fusion.1), channel_id=1, source_target_pairs={{0,4},{4,0},{8,12},{12,8},{16,20},{20,16},{24,28},{28,24},{1,5},{5... | collective-permute-start | bytes 3538952 | tf_op jit(solution)/shard_map/ppermute | solution.py:451
  408.2 15.0 %collective-permute-start.65 = (bf16[384,768]{1,0:T(8,128)(2,1)S(1)}, bf16[384,768]{1,0:T(8,128)(2,1)S(1)}, u32[]{:S(2)}, u32[]{:S(2)}) collective-permute-start(bf16[384,768]{1,0:T(8,128)(2,1)S(1)} %dynamic-slice_bitcast_fusion.2), channel_id=1, source_target_pairs={{0,8},{4,12},{8,0},{12,4},{16,24},{20,28},{24,16},{28,20},{1,9},{5... | collective-permute-start | bytes 1769480 | tf_op jit(solution)/shard_map/ppermute | solution.py:451
  423.5 20.0 %collective-permute-start.68 = (bf16[192,1536]{1,0:T(8,128)(2,1)S(1)}, bf16[192,1536]{1,0:T(8,128)(2,1)}, u32[]{:S(2)}, u32[]{:S(2)}) collective-permute-start(bf16[192,1536]{1,0:T(8,128)(2,1)S(1)} %pad_maximum_fusion.6), channel_id=1, source_target_pairs={{0,4},{4,0},{8,12},{12,8},{16,20},{20,16},{24,28},{28,24},{1,5},{5... | collective-permute-start | bytes 1769480 | tf_op jit(solution)/shard_map/ppermute | solution.py:451
  424.7 18.8 %collective-permute-start.67 = (bf16[192,1536]{1,0:T(8,128)(2,1)S(1)}, bf16[192,1536]{1,0:T(8,128)(2,1)S(1)}, u32[]{:S(2)}, u32[]{:S(2)}) collective-permute-start(bf16[192,1536]{1,0:T(8,128)(2,1)S(1)} %pad_maximum_fusion.5), channel_id=1, source_target_pairs={{0,2},{1,3},{2,0},{3,1},{4,6},{5,7},{6,4},{7,5},{8,10},{9,11},{10,... | collective-permute-start | bytes 1769480 | tf_op jit(solution)/shard_map/ppermute | solution.py:451
  425.7 17.8 %collective-permute-start.69 = (bf16[192,768]{1,0:T(8,128)(2,1)S(1)}, bf16[192,768]{1,0:T(8,128)(2,1)}, u32[]{:S(2)}, u32[]{:S(2)}) collective-permute-start(bf16[192,768]{1,0:T(8,128)(2,1)S(1)} %dynamic-slice_bitcast_fusion.4), channel_id=1, source_target_pairs={{0,16},{4,20},{8,24},{12,28},{16,0},{20,4},{24,8},{28,12},{1,17},{... | collective-permute-start | bytes 884744 | tf_op jit(solution)/shard_map/ppermute | solution.py:451
  (154 other events, 1033.2 us)
